TPU v7x, 256 devices: a whole 4x4x8 slice. The times are simulated.
256 devices in a mesh: seq: 16 (over x_lo, y, core), dp: 16 (over x_hi, z).
Axes of the slice: x: 4 (x_hi: 2, x_lo: 2; x = x_hi * 2 + x_lo), y: 4, z: 8, core: 2. Of those that a mesh axis runs over, the one named last changes fastest.
Arguments:
- normed: bfloat16 [16, 4096, 8192], P('dp', 'seq'), may hold values from -6 to 6
- query_frozen: bfloat16 [16, 4096, 4096], P('dp', 'seq'), may hold values from -64 to 64
- key_projected: bfloat16 [16, 4096, 512], P('dp', 'seq'), may hold values from -4.5 to 4.5
- value_frozen: bfloat16 [16, 4096, 512], P('dp', 'seq'), may hold values from -6 to 6
- query_down_weight: bfloat16 [8192, 16], replicated, may hold values from -0.0625 to 0.0625
- query_up_weight: bfloat16 [16, 4096], replicated, may hold values from -1.5 to 1.5
- value_down_weight: bfloat16 [8192, 16], replicated, may hold values from -0.0625 to 0.0625
- value_up_weight: bfloat16 [16, 512], replicated, may hold values from -1.5 to 1.5
- output_cotangent: bfloat16 [16, 4096, 4096], P('dp', 'seq'), may hold values from -6 to 6
Outputs:
- attn_output: bfloat16 [16, 4096, 4096], P('dp', 'seq')
- grad_aq: float32 [8192, 16], replicated
- grad_bq: float32 [16, 4096], replicated
- grad_av: float32 [8192, 16], replicated
- grad_bv: float32 [16, 512], replicated
All inputs are finite; a program needn't handle non-finite values.
Results may differ from a plain program's by a relative error of at most 0.012.
The roundings to bfloat16 on the way count: a program that leaves them out, or rounds other values in their place, can miss the bound.
Values may be sent and summed in bfloat16 or wider, within the bound.
No kernel may reach another device: no remote copies, remote signals or barrier semaphores. Data moves between devices by JAX's collectives and lax.ppermute only.
A program may use at most 64 MiB of HBM per device.

v0:
```python
import functools
import math

import jax
import jax.numpy as jnp
from jax import lax
from jax.experimental import pallas as pl
from jax.experimental.pallas import tpu as pltpu
from jax.sharding import PartitionSpec as P

QUERY_HEADS = 32
KEY_VALUE_HEADS = 4
PER_KEY = 8
WIDTH = 128
RANK = 16
adapter_scale = 2.0
masked_score = -1e30
AXES = ("seq", "dp")
CORE_BIT = 16
PLANE_BITS = (32, 64, 128, 8)
DEPTH_BITS = (1, 2, 4)
CHUNKS = 32
CHUNK_ROWS = 96
NT = (((1,), (1,)), ((), ()))
F32 = jnp.float32
BF16 = jnp.bfloat16
STACK = 4
VMEM_LIMIT = 48 * 1024 * 1024


def groups_of(bits, count):
    groups = []
    for base in range(count):
        if any(base & bit for bit in bits):
            continue
        members = []
        for code in range(1 << len(bits)):
            members.append(base + sum(bit for n, bit in enumerate(bits) if code >> n & 1))
        groups.append(members)
    return groups


def exchanged(value, bits):
    groups = groups_of(bits, lax.axis_size(AXES))
    return lax.all_to_all(value, AXES, 0, 0, axis_index_groups=groups)


def sum_over_first(value):
    return jnp.sum(value.astype(jnp.float32), axis=0)


def spread(value, bits):
    copies = jnp.broadcast_to(value[None], (1 << len(bits),) + value.shape)
    return exchanged(copies, bits)


def swapped(value, bit):
    count = lax.axis_size(AXES)
    return lax.ppermute(value, AXES, [(i, i ^ bit) for i in range(count)])


def shifted(value, axis, by):
    devices = lax.axis_size(axis)
    return lax.ppermute(value, axis, [(i, (i + by) % devices) for i in range(devices)])


def dot_nt(a, b):
    return lax.dot_general(a, b, NT, preferred_element_type=F32)


def dot(a, b):
    return jnp.dot(a, b, preferred_element_type=F32)


def latent_kernel(steps, place_ref, x_ref, dq_ref, dv_ref, k_ref, vf_ref, upv_ref, lat_ref, latt_ref, value_ref, send_ref, acc):
    step = pl.program_id(0)
    down = jnp.concatenate([dq_ref[...], dv_ref[...]], axis=0)
    part = dot_nt(x_ref[...], down)

    @pl.when(step == 0)
    def _():
        acc[...] = part

    @pl.when(step > 0)
    def _():
        acc[...] += part

    @pl.when(step == steps - 1)
    def _():
        whole = acc[...]
        lat = whole.astype(BF16)
        lat_ref[...] = lat
        latt_ref[...] = whole.T.astype(BF16)
        up = dot(lat[:, RANK:], upv_ref[...])
        value_ref[...] = (vf_ref[...].astype(F32) + adapter_scale * up).astype(BF16)
        half = value_ref.shape[1] // 2
        sent = pl.ds(pl.multiple_of(place_ref[0] * half, half), half)
        send_ref[:, :half] = k_ref[:, sent]
        send_ref[:, half:] = value_ref[:, sent]


def latents(place, x, down_q, down_v, keys, value_frozen, up_v, steps=8):
    tokens, model = x.shape
    block = model // steps
    cols = value_frozen.shape[1]
    along = lambda i, s: (0, i)
    whole = lambda i, s: (0, 0)
    return pl.pallas_call(
        functools.partial(latent_kernel, steps),
        grid_spec=pltpu.PrefetchScalarGridSpec(
            num_scalar_prefetch=1,
            grid=(steps,),
            in_specs=[
                pl.BlockSpec((tokens, block), along),
                pl.BlockSpec((RANK, block), along),
                pl.BlockSpec((RANK, block), along),
                pl.BlockSpec((tokens, cols), whole),
                pl.BlockSpec((tokens, cols), whole),
                pl.BlockSpec((RANK, cols), whole),
            ],
            out_specs=[
                pl.BlockSpec((tokens, 2 * RANK), whole),
                pl.BlockSpec((2 * RANK, tokens), whole),
                pl.BlockSpec((tokens, cols), whole),
                pl.BlockSpec((tokens, cols), whole),
            ],
            scratch_shapes=[pltpu.VMEM((tokens, 2 * RANK), F32)],
        ),
        out_shape=[
            jax.ShapeDtypeStruct((tokens, 2 * RANK), BF16),
            jax.ShapeDtypeStruct((2 * RANK, tokens), BF16),
            jax.ShapeDtypeStruct((tokens, cols), BF16),
            jax.ShapeDtypeStruct((tokens, cols), BF16),
        ],
        compiler_params=pltpu.CompilerParams(vmem_limit_bytes=VMEM_LIMIT),
        cost_estimate=pl.CostEstimate(
            flops=2 * tokens * model * 2 * RANK, bytes_accessed=2 * tokens * model, transcendentals=0
        ),
        name="latents",
    )(place, x, down_q, down_v, keys, value_frozen, up_v)


def attend_kernel(far, chained, first_ref, *refs):
    refs = list(refs)
    qf_ref, do_ref, k_ref, v_ref = refs[:4]
    refs = refs[4:]
    if far:
        kp_ref, vp_ref = refs[:2]
        refs = refs[2:]
    lat_ref, latt_ref, upq_ref = refs[:3]
    refs = refs[3:]
    if chained:
        up_in = refs[2]
        refs = refs[3:]
    out_ref, bq_ref, upt_ref, dv_ref = refs[:4]
    refs = refs[4:]
    if far:
        dvp_ref = refs[0]
        refs = refs[1:]
    q_scr, dq_scr = refs

    tokens = qf_ref.shape[0]
    root = 1.0 / math.sqrt(WIDTH)
    base2 = root * math.log2(math.e)
    lat = lat_ref[:, :RANK]
    q_scr[...] = (qf_ref[...].astype(F32) + adapter_scale * dot(lat, upq_ref[...])).astype(BF16)
    if far:
        keys = jnp.concatenate([kp_ref[...], k_ref[...]], axis=0)
        values = jnp.concatenate([vp_ref[...], v_ref[...]], axis=0)
    else:
        keys = k_ref[...]
        values = v_ref[...]
    row = lax.broadcasted_iota(jnp.int32, (STACK * tokens, tokens), 0) % tokens
    col = lax.broadcasted_iota(jnp.int32, (STACK * tokens, tokens), 1)
    seen = col <= row
    dvt = None
    for block in range(PER_KEY // STACK):
        slices = [slice((block * STACK + n) * WIDTH, (block * STACK + n + 1) * WIDTH) for n in range(STACK)]
        q = jnp.concatenate([q_scr[:, cols] for cols in slices], axis=0)
        do = jnp.concatenate([do_ref[:, cols] for cols in slices], axis=0)
        score = dot_nt(q, keys)
        own = jnp.where(seen, score[:, -tokens:], masked_score)
        if far:
            score = jnp.concatenate([score[:, :tokens], own], axis=1)
        else:
            score = own
        top = jnp.max(score, axis=1, keepdims=True)
        expo = jnp.exp2((score - top) * base2)
        prob = expo * (1.0 / jnp.sum(expo, axis=1, keepdims=True))
        prob_b = prob.astype(BF16)
        attended = dot(prob_b, values)
        delta = jnp.sum(do.astype(F32) * attended, axis=1, keepdims=True)
        dprob = dot_nt(do, values)
        dscore = (prob * (dprob - delta)).astype(BF16)
        dq_rows = (dot(dscore, keys) * root).astype(BF16)
        for n, cols in enumerate(slices):
            rows = slice(n * tokens, (n + 1) * tokens)
            out_ref[:, cols] = attended[rows].astype(BF16)
            dq_scr[:, cols] = dq_rows[rows]
        term = lax.dot_general(do, prob_b, (((0,), (0,)), ((), ())), preferred_element_type=F32)
        dvt = term if dvt is None else dvt + term
    dv = dvt.T
    dv_ref[...] = dv[-tokens:]
    if far:
        dvp_ref[...] = dv[:tokens].astype(dvp_ref.dtype)
    dq = dq_scr[...]
    bq_ref[...] = dot(latt_ref[:RANK, :], dq)
    up = dot_nt(upq_ref[...], dq)
    step = pl.program_id(0)

    @pl.when(step == 0)
    def _():
        upt_ref[...] = up + up_in[...] if chained else up

    @pl.when(step > 0)
    def _():
        upt_ref[...] += up


def attend(first, groups, query_frozen, dout, keys, values, prev, lat, latt, up_q, chain):
    tokens = query_frozen.shape[0]
    far = prev is not None
    chained = chain is not None
    wide = PER_KEY * WIDTH
    at_group = lambda i, s: (0, s[0] + i)
    at_step = lambda i, s: (0, i)
    whole = lambda i, s: (0, 0)
    args = [query_frozen, dout, keys, values]
    specs = [
        pl.BlockSpec((tokens, wide), at_group),
        pl.BlockSpec((tokens, wide), at_group),
        pl.BlockSpec((tokens, WIDTH), at_group),
        pl.BlockSpec((tokens, WIDTH), at_group),
    ]
    if far:
        args += [prev, prev]
        specs += [
            pl.BlockSpec((tokens, WIDTH), at_step),
            pl.BlockSpec((tokens, WIDTH), lambda i, s: (0, groups + i)),
        ]
    args += [lat, latt, up_q]
    specs += [
        pl.BlockSpec((tokens, 2 * RANK), whole),
        pl.BlockSpec((2 * RANK, tokens), whole),
        pl.BlockSpec((RANK, wide), at_group),
    ]
    aliases = {}
    if chained:
        aliases = {1 + len(args): 0, 2 + len(args): 1}
        args += list(chain)
        specs += [pl.BlockSpec(memory_space=pl.ANY)] * 2 + [pl.BlockSpec((RANK, tokens), whole)]
    out_specs = [
        pl.BlockSpec((tokens, wide), at_group),
        pl.BlockSpec((RANK, wide), at_group),
        pl.BlockSpec((RANK, tokens), whole),
        pl.BlockSpec((tokens, WIDTH), at_step),
    ]
    out_shape = [
        jax.ShapeDtypeStruct(query_frozen.shape, BF16),
        jax.ShapeDtypeStruct(up_q.shape, F32),
        jax.ShapeDtypeStruct((RANK, tokens), F32),
        jax.ShapeDtypeStruct((tokens, groups * WIDTH), F32),
    ]
    if far:
        out_specs.append(pl.BlockSpec((tokens, WIDTH), at_step))
        out_shape.append(jax.ShapeDtypeStruct((tokens, groups * WIDTH), BF16))
    span = tokens * (2 if far else 1)
    return pl.pallas_call(
        functools.partial(attend_kernel, far, chained),
        grid_spec=pltpu.PrefetchScalarGridSpec(
            num_scalar_prefetch=1,
            grid=(groups,),
            in_specs=specs,
            out_specs=out_specs,
            scratch_shapes=[pltpu.VMEM((tokens, wide), BF16), pltpu.VMEM((tokens, wide), BF16)],
        ),
        out_shape=out_shape,
        input_output_aliases=aliases,
        compiler_params=pltpu.CompilerParams(vmem_limit_bytes=VMEM_LIMIT),
        cost_estimate=pl.CostEstimate(
            flops=groups * 10 * tokens * span * wide,
            bytes_accessed=groups * 6 * tokens * wide,
            transcendentals=groups * PER_KEY * tokens * span,
        ),
        name="attend_far" if far else "attend_near",
    )(first, *args)


def outer_kernel(fresh, half_ref, *refs):
    refs = list(refs)
    x_ref, bq_ref, latt_ref, dv_ref = refs[:4]
    refs = refs[4:]
    if fresh:
        upt_ref, near_ref, back_ref, upv_far, upv_near, out_ref, both_ref, near_out, bv_scr = refs
    else:
        both_ref, out_ref, bv_scr = refs
    step = pl.program_id(0)

    @pl.when(step == 0)
    def _():
        dvb = dv_ref[...].astype(BF16)
        bv_scr[...] = dot(latt_ref[RANK:, :], dvb)
        if fresh:
            near = (near_ref[...] + back_ref[...].astype(F32)).astype(BF16)
            near_out[...] = near
            upv = dot_nt(upv_far[...], dvb) + dot_nt(upv_near[...], near)
            both_ref[...] = jnp.concatenate([upt_ref[...], upv], axis=0).astype(BF16)

    part = dot(both_ref[...], x_ref[...])
    for chunk in range(out_ref.shape[0]):
        for lane in range(2):
            cols = slice((2 * chunk + lane) * WIDTH, (2 * chunk + lane + 1) * WIDTH)
            rows = slice(lane * RANK, (lane + 1) * RANK)
            out_ref[chunk, rows, :] = part[:RANK, cols].astype(out_ref.dtype)
            rows = slice((2 + lane) * RANK, (3 + lane) * RANK)
            out_ref[chunk, rows, :] = part[RANK:, cols].astype(out_ref.dtype)
        cols = slice(chunk * WIDTH, (chunk + 1) * WIDTH)
        out_ref[chunk, 4 * RANK : 5 * RANK, :] = bq_ref[:, cols].astype(out_ref.dtype)
        out_ref[chunk, 5 * RANK :, :] = jnp.zeros((RANK, WIDTH), out_ref.dtype)

    @pl.when(step == 0)
    def _():
        for chunk in range(2):
            cols = slice(chunk * WIDTH, (chunk + 1) * WIDTH)
            out_ref[chunk, 5 * RANK :, :] = bv_scr[:, cols].astype(out_ref.dtype)


def outer(half, x, bq, latt, dv, dtype, fresh=None, both=None, steps=4):
    tokens, model = x.shape
    per_step = CHUNKS // 2 // steps
    along = lambda i, s: (0, s[0] * steps + i)
    whole = lambda i, s: (0, 0)
    cols = dv.shape[1]
    args = [x, bq, latt, dv]
    specs = [
        pl.BlockSpec((tokens, per_step * 2 * WIDTH), along),
        pl.BlockSpec((RANK, per_step * WIDTH), along),
        pl.BlockSpec((2 * RANK, tokens), whole),
        pl.BlockSpec((tokens, cols), whole),
    ]
    out_specs = [pl.BlockSpec((per_step, CHUNK_ROWS, WIDTH), lambda i, s: (i, 0, 0))]
    out_shape = [jax.ShapeDtypeStruct((CHUNKS // 2, CHUNK_ROWS, WIDTH), dtype)]
    if fresh is not None:
        upt, near, back, up_v = fresh
        args += [upt, near, back, up_v, up_v]
        specs += [
            pl.BlockSpec((RANK, tokens), whole),
            pl.BlockSpec((tokens, cols), whole),
            pl.BlockSpec((tokens, cols), whole),
            pl.BlockSpec((RANK, cols), lambda i, s: (0, s[0])),
            pl.BlockSpec((RANK, cols), lambda i, s: (0, 1 - s[0])),
        ]
        out_specs += [pl.BlockSpec((2 * RANK, tokens), whole), pl.BlockSpec((tokens, cols), whole)]
        out_shape += [
            jax.ShapeDtypeStruct((2 * RANK, tokens), BF16),
            jax.ShapeDtypeStruct((tokens, cols), BF16),
        ]
    else:
        args.append(both)
        specs.append(pl.BlockSpec((2 * RANK, tokens), whole))
    return pl.pallas_call(
        functools.partial(outer_kernel, fresh is not None),
        grid_spec=pltpu.PrefetchScalarGridSpec(
            num_scalar_prefetch=1,
            grid=(steps,),
            in_specs=specs,
            out_specs=out_specs,
            scratch_shapes=[pltpu.VMEM((RANK, cols), F32)],
        ),
        out_shape=out_shape,
        compiler_params=pltpu.CompilerParams(vmem_limit_bytes=VMEM_LIMIT),
        cost_estimate=pl.CostEstimate(
            flops=2 * tokens * model * RANK, bytes_accessed=tokens * model, transcendentals=0
        ),
        name="outer_first" if fresh is not None else "outer_second",
    )(half, *args)


def unpack_kernel(scale, half_ref, own_ref, other_ref, aq_ref, av_ref, bq_ref, bv_ref):
    def fill(ref):
        for chunk in range(CHUNKS // 2):
            for lane in range(2):
                cols = slice((2 * chunk + lane) * WIDTH, (2 * chunk + lane + 1) * WIDTH)
                rows = slice(lane * RANK, (lane + 1) * RANK)
                aq_ref[:, cols] = ref[chunk, rows, :].astype(F32) * scale
                rows = slice((2 + lane) * RANK, (3 + lane) * RANK)
                av_ref[:, cols] = ref[chunk, rows, :].astype(F32) * scale
            cols = slice(chunk * WIDTH, (chunk + 1) * WIDTH)
            bq_ref[:, cols] = ref[chunk, 4 * RANK : 5 * RANK, :].astype(F32) * scale
            if chunk < 2:
                bv_ref[:, cols] = ref[chunk, 5 * RANK :, :].astype(F32) * scale

    @pl.when(pl.program_id(0) == 0)
    def _():
        fill(own_ref)

    @pl.when(pl.program_id(0) == 1)
    def _():
        fill(other_ref)


def unpacked(half, own, other, scale, shapes):
    flip = lambda i, s: (0, (s[0] + i) % 2)
    whole = lambda i, s: (0, 0, 0)
    return pl.pallas_call(
        functools.partial(unpack_kernel, scale),
        grid_spec=pltpu.PrefetchScalarGridSpec(
            num_scalar_prefetch=1,
            grid=(2,),
            in_specs=[pl.BlockSpec(own.shape, whole)] * 2,
            out_specs=[pl.BlockSpec((rows, cols // 2), flip) for rows, cols in shapes],
        ),
        out_shape=[jax.ShapeDtypeStruct(shape, F32) for shape in shapes],
        compiler_params=pltpu.CompilerParams(vmem_limit_bytes=VMEM_LIMIT),
        cost_estimate=pl.CostEstimate(flops=0, bytes_accessed=3 * 1024 * 1024, transcendentals=0),
        name="unpack",
    )(half, own, other)


def summed(given, kept):
    halves = kept + swapped(given, CORE_BIT).astype(F32)
    piece = sum_over_first(exchanged(halves.astype(BF16), PLANE_BITS))
    piece = sum_over_first(spread(piece.astype(BF16), DEPTH_BITS))
    return spread(piece.astype(BF16), PLANE_BITS)


def on_device(
    normed,
    query_frozen,
    key_projected,
    value_frozen,
    query_down_weight,
    query_up_weight,
    value_down_weight,
    value_up_weight,
    output_cotangent,
):
    x, qf, keys, vf, dout = [
        a[0] for a in (normed, query_frozen, key_projected, value_frozen, output_cotangent)
    ]
    tokens = x.shape[0]
    parity = lax.axis_index("seq") % 2
    place = parity.reshape(1).astype(jnp.int32)
    away = 1 - place
    pair = KEY_VALUE_HEADS // 2
    lat, latt, values, sent = latents(
        place, x, query_down_weight.T, value_down_weight.T, keys, vf, value_up_weight
    )
    prev = shifted(sent, "seq", 1)
    out, bq, upt, dv_near = attend(
        pair * place, pair, qf, dout, keys, values, None, lat, latt, query_up_weight, None
    )
    out, bq, upt, dv_far, dv_back = attend(
        pair * away, pair, qf, dout, keys, values, prev, lat, latt, query_up_weight, (out, bq, upt)
    )
    back = shifted(dv_back, "seq", -1)
    given, both, near = outer(
        away, x, bq, latt, dv_far, BF16, fresh=(upt, dv_near, back, value_up_weight)
    )
    (kept,) = outer(place, x, bq, latt, near, F32, both=both)
    own_half = summed(given, kept)
    other_half = swapped(own_half, CORE_BIT)
    scale_factor = adapter_scale / math.sqrt(tokens * lax.axis_size("seq") * lax.axis_size("dp"))
    model = x.shape[1]
    shapes = [(RANK, model), (RANK, model), (RANK, qf.shape[1]), (RANK, vf.shape[1])]
    aq, av, bq_sum, bv_sum = unpacked(place, own_half, other_half, scale_factor, shapes)
    return (out[None], aq.T, bq_sum, av.T, bv_sum)


def solution(mesh):
    in_specs = (
        P("dp", "seq", None),
        P("dp", "seq", None),
        P("dp", "seq", None),
        P("dp", "seq", None),
        P(),
        P(),
        P(),
        P(),
        P("dp", "seq", None),
    )
    out_specs = (P("dp", "seq", None), P(), P(), P(), P())
    return jax.shard_map(
        on_device, mesh=mesh, in_specs=in_specs, out_specs=out_specs, check_vma=False
    )
```

profile of v0, /device:TPU:1, one launch (start us, length us, event | category | flops | bytes accessed | tf_op | source)
XLA Modules:
  0.0 87.2 jit_solution(10640081784689312587)
XLA Ops:
  0.7 2.2 %copy-done = bf16[1,256,8192]{2,1,0:T(8,128)(2,1)S(1)} copy-done((bf16[1,256,8192]{2,1,0:T(8,128)(2,1)S(1)}, bf16[1,256,8192]{2,1,0:T(8,128)(2,1)}, u32[]{:S(2)}) %copy-start) | copy-done | bytes 4194328
  2.8 0.9 %copy-done.2 = bf16[8192,16]{0,1:T(8,128)(2,1)S(1)} copy-done((bf16[8192,16]{0,1:T(8,128)(2,1)S(1)}, bf16[8192,16]{0,1:T(8,128)(2,1)}, u32[]{:S(2)}) %copy-start.2) | copy-done | bytes 262168
  3.8 0.9 %copy-done.3 = bf16[8192,16]{0,1:T(8,128)(2,1)S(1)} copy-done((bf16[8192,16]{0,1:T(8,128)(2,1)S(1)}, bf16[8192,16]{0,1:T(8,128)(2,1)}, u32[]{:S(2)}) %copy-start.3) | copy-done | bytes 262168
  4.7 0.9 %copy-done.4 = bf16[1,256,512]{2,1,0:T(8,128)(2,1)S(1)} copy-done((bf16[1,256,512]{2,1,0:T(8,128)(2,1)S(1)}, bf16[1,256,512]{2,1,0:T(8,128)(2,1)}, u32[]{:S(2)}) %copy-start.4) | copy-done | bytes 262168
  5.7 0.9 %copy-done.5 = bf16[1,256,512]{2,1,0:T(8,128)(2,1)S(1)} copy-done((bf16[1,256,512]{2,1,0:T(8,128)(2,1)S(1)}, bf16[1,256,512]{2,1,0:T(8,128)(2,1)}, u32[]{:S(2)}) %copy-start.5) | copy-done | bytes 262168
  6.6 0.7 copy-done.7
  7.4 3.0 %latents.1 = (bf16[256,32]{1,0:T(8,128)(2,1)S(1)}, bf16[32,256]{1,0:T(8,128)(2,1)S(1)}, bf16[256,512]{1,0:T(8,128)(2,1)S(1)}, bf16[256,512]{1,0:T(8,128)(2,1)S(1)}) custom-call(s32[1]{0:T(128)} %bitcast.place_ref.half_ref, bf16[256,8192]{1,0:T(8,128)(2,1)S(1)} %bitcast.11, bf16[16,8192]{1,0:T(8,128)(2,1)S(1)} %bitcast.14, bf16[16,8192]{1,0:T(8,128)(2,1)S(1)} %bitcast.15, ...), custom_call_target="tpu_custom_call" | custom-call | flops 134217728 | bytes 4194304 | tf_op jit(solution)/shard_map/latents/pallas_call | solution.py:108
  10.4 2.8 %collective-permute-start = (bf16[256,512]{1,0:T(8,128)(2,1)S(1)}, bf16[256,512]{1,0:T(8,128)(2,1)S(1)}, u32[]{:S(2)}, u32[]{:S(2)}) collective-permute-start(bf16[256,512]{1,0:T(8,128)(2,1)S(1)} %get-tuple-element.26), channel_id=1, source_target_pairs={{0,16},{16,32},{32,48},{48,64},{64,80},{80,96},{96,112},{112,128},... | collective-permute-start | bytes 786440 | tf_op jit(solution)/shard_map/ppermute | solution.py:64
  13.2 6.0 %attend_near.1 = (bf16[256,4096]{1,0:T(8,128)(2,1)}, f32[16,4096]{1,0:T(8,128)S(1)}, f32[16,256]{1,0:T(8,128)S(1)}, f32[256,256]{1,0:T(8,128)S(1)}) custom-call(s32[1]{0:T(128)S(6)} %mul.7.first_ref, bf16[256,4096]{1,0:T(8,128)(2,1)S(1)} %bitcast.20, bf16[256,4096]{1,0:T(8,128)(2,1)S(1)} %bitcast.22, bf16[256,512]{1,0:T(8,128)(2,1)S(1)} %bitcast.18, ...), custom_call_target="tpu_custom_call" | custom-call | flops 1342177280 | bytes 3145728 | tf_op jit(solution)/shard_map/attend_near/pallas_call | solution.py:268
  19.1 8.6 %attend_far.1 = (bf16[256,4096]{1,0:T(8,128)(2,1)}, f32[16,4096]{1,0:T(8,128)S(1)}, f32[16,256]{1,0:T(8,128)S(1)}, f32[256,256]{1,0:T(8,128)S(1)}, bf16[256,256]{1,0:T(8,128)(2,1)S(1)}) custom-call(s32[1]{0:T(128)S(6)} %mul.6.first_ref, bf16[256,4096]{1,0:T(8,128)(2,1)S(1)} %bitcast.21, ...), custom_call_target="tpu_custom_call", output_to_operand_aliasing={{0}: (10, {}), {1}: (11, {})} | custom-call | flops 2684354560 | bytes 3145728 | tf_op jit(solution)/shard_map/attend_far/pallas_call | solution.py:268
  27.7 2.4 %collective-permute-start.1 = (bf16[256,256]{1,0:T(8,128)(2,1)S(1)}, bf16[256,256]{1,0:T(8,128)(2,1)S(1)}, u32[]{:S(2)}, u32[]{:S(2)}) collective-permute-start(bf16[256,256]{1,0:T(8,128)(2,1)S(1)} %get-tuple-element.37), channel_id=1, source_target_pairs={{0,240},{16,0},{32,16},{48,32},{64,48},{80,64},{96,80},{112,96},{1... | collective-permute-start | bytes 393224 | tf_op jit(solution)/shard_map/ppermute | solution.py:64
  30.1 2.0 %collective-permute-done.1.refs_6_ = bf16[256,256]{1,0:T(8,128)(2,1)S(1)} collective-permute-done((bf16[256,256]{1,0:T(8,128)(2,1)S(1)}, bf16[256,256]{1,0:T(8,128)(2,1)S(1)}, u32[]{:S(2)}, u32[]{:S(2)}) %collective-permute-start.1) | collective-permute-done | bytes 131104 | tf_op jit(solution)/shard_map/ppermute | solution.py:64
  32.1 1.2 %outer_first.1 = (bf16[16,96,128]{2,1,0:T(8,128)(2,1)S(1)}, bf16[32,256]{1,0:T(8,128)(2,1)S(1)}, bf16[256,256]{1,0:T(8,128)(2,1)S(1)}) custom-call(s32[1]{0:T(128)S(6)} %sub.3.half_ref, bf16[256,8192]{1,0:T(8,128)(2,1)S(1)} %bitcast.12, f32[16,4096]{1,0:T(8,128)S(1)} %get-tuple-element.33.refs_1_, ...), custom_call_target="tpu_custom_call" | custom-call | flops 67108864 | bytes 2097152 | tf_op jit(solution)/shard_map/outer_first/pallas_call | solution.py:361
  33.4 2.6 %collective-permute-start.2 = (bf16[16,96,128]{2,1,0:T(8,128)(2,1)S(1)}, bf16[16,96,128]{2,1,0:T(8,128)(2,1)S(1)}, u32[]{:S(2)}, u32[]{:S(2)}) collective-permute-start(bf16[16,96,128]{2,1,0:T(8,128)(2,1)S(1)} %get-tuple-element.40), channel_id=1, source_target_pairs={{0,16},{1,17},{2,18},{3,19},{4,20},{5,21},{6,22},{7,23},{8,24},{9,... | collective-permute-start | bytes 1179656 | tf_op jit(solution)/shard_map/ppermute | solution.py:59
  36.0 1.1 %outer_second.1 = f32[16,96,128]{2,1,0:T(8,128)S(1)} custom-call(s32[1]{0:T(128)} %bitcast.place_ref.half_ref, bf16[256,8192]{1,0:T(8,128)(2,1)S(1)} %bitcast.13, f32[16,4096]{1,0:T(8,128)S(1)} %get-tuple-element.33.refs_1_, bf16[32,256]{1,0:T(8,128)(2,1)S(1)} %get-tuple-element.28.refs_5_.refs_7_.refs_2_, bf16[256,256]{1,0:T(8,128)(2,1)S(1)} %get-tuple-element.38.refs_3_, ...), custom_call_target="tpu_custom_call" | custom-call | flops 67108864 | bytes 2097152 | tf_op jit(solution)/shard_map/outer_second/pallas_call | solution.py:361
  37.1 0.2 collective-permute-done.2
  37.3 0.1 add_convert_fusion
  37.4 14.9 %all_to_all.15 = bf16[16,96,128]{2,1,0:T(8,128)(2,1)S(1)} all-to-all(bf16[16,96,128]{2,1,0:T(8,128)(2,1)S(1)} %add_convert_fusion), channel_id=1, replica_groups={{0,32,64,96,128,160,192,224,8,40,72,104,136,168,200,232},{1,33,65,97,12..., dimensions={0} | all-to-all | bytes 786432 | tf_op jit(solution)/shard_map/all_to_all | solution.py:45
  52.3 0.1 reduce_sum.24
  52.4 16.6 %all_to_all.16 = bf16[8,96,128]{2,1,0:T(8,128)(2,1)S(1)} all-to-all(bf16[8,96,128]{2,1,0:T(8,128)(2,1)S(1)} %broadcast_in_dim.7), channel_id=1, replica_groups={{0,1,2,3,4,5,6,7},{8,9,10,11,12,13,14,15},{16,17,18,19,20,21,22,23},{24..., dimensions={0} | all-to-all | bytes 393216 | tf_op jit(solution)/shard_map/all_to_all | solution.py:45
  69.1 11.3 %all_to_all.17.own_ref = bf16[16,96,128]{2,1,0:T(8,128)(2,1)S(1)} all-to-all(bf16[16,96,128]{2,1,0:T(8,128)(2,1)S(1)} %broadcast_in_dim.8), channel_id=1, replica_groups={{0,32,64,96,128,160,192,224,8,40,72,104,136,168,200,232},{1,33,65,97,12..., dimensions={0} | all-to-all | bytes 786432 | tf_op jit(solution)/shard_map/all_to_all | solution.py:45
  80.5 4.3 %collective-permute-start.3 = (bf16[16,96,128]{2,1,0:T(8,128)(2,1)S(1)}, bf16[16,96,128]{2,1,0:T(8,128)(2,1)S(1)}, u32[]{:S(2)}, u32[]{:S(2)}) collective-permute-start(bf16[16,96,128]{2,1,0:T(8,128)(2,1)S(1)} %all_to_all.17.own_ref), channel_id=1, source_target_pairs={{0,16},{1,17},{2,18},{3,19},{4,20},{5,21},{6,22},{7,23},{8,24},{9,... | collective-permute-start | bytes 1179656 | tf_op jit(solution)/shard_map/ppermute | solution.py:59
  84.8 1.3 %collective-permute-done.3.other_ref = bf16[16,96,128]{2,1,0:T(8,128)(2,1)S(1)} collective-permute-done((bf16[16,96,128]{2,1,0:T(8,128)(2,1)S(1)}, bf16[16,96,128]{2,1,0:T(8,128)(2,1)S(1)}, u32[]{:S(2)}, u32[]{:S(2)}) %collective-permute-start.3) | collective-permute-done | bytes 393248 | tf_op jit(solution)/shard_map/ppermute | solution.py:59
  86.1 1.1 %unpack.1 = (f32[16,8192]{1,0:T(8,128)}, f32[16,8192]{1,0:T(8,128)}, f32[16,4096]{1,0:T(8,128)}, f32[16,512]{1,0:T(8,128)}) custom-call(s32[1]{0:T(128)} %bitcast.place_ref.half_ref, bf16[16,96,128]{2,1,0:T(8,128)(2,1)S(1)} %all_to_all.17.own_ref, bf16[16,96,128]{2,1,0:T(8,128)(2,1)S(1)} %collective-permute-done.3.other_ref), custom_call_target="tpu_custom_call" | custom-call | bytes 3145728 | tf_op jit(solution)/shard_map/unpack/pallas_call | solution.py:405
  (22 shorter events, 0.1 us)
Async XLA Ops:
  0.6 2.2 %copy-start = (bf16[1,256,8192]{2,1,0:T(8,128)(2,1)S(1)}, bf16[1,256,8192]{2,1,0:T(8,128)(2,1)}, u32[]{:S(2)}) copy-start(bf16[1,256,8192]{2,1,0:T(8,128)(2,1)} %param.9) | copy-start | bytes 12582916
  2.8 0.9 %copy-start.2 = (bf16[8192,16]{0,1:T(8,128)(2,1)S(1)}, bf16[8192,16]{0,1:T(8,128)(2,1)}, u32[]{:S(2)}) copy-start(bf16[8192,16]{0,1:T(8,128)(2,1)} %param.13) | copy-start | bytes 786436
  3.8 0.9 %copy-start.3 = (bf16[8192,16]{0,1:T(8,128)(2,1)S(1)}, bf16[8192,16]{0,1:T(8,128)(2,1)}, u32[]{:S(2)}) copy-start(bf16[8192,16]{0,1:T(8,128)(2,1)} %param.15) | copy-start | bytes 786436
  4.7 0.9 %copy-start.4 = (bf16[1,256,512]{2,1,0:T(8,128)(2,1)S(1)}, bf16[1,256,512]{2,1,0:T(8,128)(2,1)}, u32[]{:S(2)}) copy-start(bf16[1,256,512]{2,1,0:T(8,128)(2,1)} %param.12) | copy-start | bytes 786436
  5.7 0.9 %copy-start.5 = (bf16[1,256,512]{2,1,0:T(8,128)(2,1)S(1)}, bf16[1,256,512]{2,1,0:T(8,128)(2,1)}, u32[]{:S(2)}) copy-start(bf16[1,256,512]{2,1,0:T(8,128)(2,1)} %param.11) | copy-start | bytes 786436
  6.6 0.7 copy-start.7
  7.4 5.8 %copy-start.6 = (bf16[1,256,512]{2,1,0:T(8,128)(2,1)S(1)}, bf16[1,256,512]{2,1,0:T(8,128)(2,1)}, u32[]{:S(2)}) copy-start(bf16[1,256,512]{2,1,0:T(8,128)(2,1)} %param.11) | copy-start | bytes 786436
  7.4 5.8 %copy-start.9 = (bf16[1,256,4096]{2,1,0:T(8,128)(2,1)S(1)}, bf16[1,256,4096]{2,1,0:T(8,128)(2,1)}, u32[]{:S(2)}) copy-start(bf16[1,256,4096]{2,1,0:T(8,128)(2,1)} %param.10) | copy-start | bytes 6291460
  7.4 5.8 %copy-start.10 = (bf16[1,256,4096]{2,1,0:T(8,128)(2,1)S(1)}, bf16[1,256,4096]{2,1,0:T(8,128)(2,1)}, u32[]{:S(2)}) copy-start(bf16[1,256,4096]{2,1,0:T(8,128)(2,1)} %param.17) | copy-start | bytes 6291460
  7.4 5.8 %copy-start.11 = (bf16[16,4096]{1,0:T(8,128)(2,1)S(1)}, bf16[16,4096]{1,0:T(8,128)(2,1)}, u32[]{:S(2)}) copy-start(bf16[16,4096]{1,0:T(8,128)(2,1)} %refs_8_.2) | copy-start | bytes 393220
  10.4 8.8 %collective-permute-start = (bf16[256,512]{1,0:T(8,128)(2,1)S(1)}, bf16[256,512]{1,0:T(8,128)(2,1)S(1)}, u32[]{:S(2)}, u32[]{:S(2)}) collective-permute-start(bf16[256,512]{1,0:T(8,128)(2,1)S(1)} %get-tuple-element.26), channel_id=1, source_target_pairs={{0,16},{16,32},{32,48},{48,64},{64,80},{80,96},{96,112},{112,128},... | collective-permute-start | bytes 786440 | tf_op jit(solution)/shard_map/ppermute | solution.py:64
  19.1 13.0 %copy-start.1 = (bf16[1,256,8192]{2,1,0:T(8,128)(2,1)S(1)}, bf16[1,256,8192]{2,1,0:T(8,128)(2,1)}, u32[]{:S(2)}) copy-start(bf16[1,256,8192]{2,1,0:T(8,128)(2,1)} %param.9) | copy-start | bytes 12582916
  19.1 13.0 %copy-start.8 = (bf16[16,512]{1,0:T(8,128)(2,1)S(1)}, bf16[16,512]{1,0:T(8,128)(2,1)}, u32[]{:S(2)}) copy-start(bf16[16,512]{1,0:T(8,128)(2,1)} %refs_8_.3) | copy-start | bytes 49156
  27.7 4.4 %collective-permute-start.1 = (bf16[256,256]{1,0:T(8,128)(2,1)S(1)}, bf16[256,256]{1,0:T(8,128)(2,1)S(1)}, u32[]{:S(2)}, u32[]{:S(2)}) collective-permute-start(bf16[256,256]{1,0:T(8,128)(2,1)S(1)} %get-tuple-element.37), channel_id=1, source_target_pairs={{0,240},{16,0},{32,16},{48,32},{64,48},{80,64},{96,80},{112,96},{1... | collective-permute-start | bytes 393224 | tf_op jit(solution)/shard_map/ppermute | solution.py:64
  33.4 4.0 %collective-permute-start.2 = (bf16[16,96,128]{2,1,0:T(8,128)(2,1)S(1)}, bf16[16,96,128]{2,1,0:T(8,128)(2,1)S(1)}, u32[]{:S(2)}, u32[]{:S(2)}) collective-permute-start(bf16[16,96,128]{2,1,0:T(8,128)(2,1)S(1)} %get-tuple-element.40), channel_id=1, source_target_pairs={{0,16},{1,17},{2,18},{3,19},{4,20},{5,21},{6,22},{7,23},{8,24},{9,... | collective-permute-start | bytes 1179656 | tf_op jit(solution)/shard_map/ppermute | solution.py:59
  80.5 5.6 %collective-permute-start.3 = (bf16[16,96,128]{2,1,0:T(8,128)(2,1)S(1)}, bf16[16,96,128]{2,1,0:T(8,128)(2,1)S(1)}, u32[]{:S(2)}, u32[]{:S(2)}) collective-permute-start(bf16[16,96,128]{2,1,0:T(8,128)(2,1)S(1)} %all_to_all.17.own_ref), channel_id=1, source_target_pairs={{0,16},{1,17},{2,18},{3,19},{4,20},{5,21},{6,22},{7,23},{8,24},{9,... | collective-permute-start | bytes 1179656 | tf_op jit(solution)/shard_map/ppermute | solution.py:59
where the time goes:
time: 87.6 us; the launch traced here: 87.2 us
  blocking collectives  42.9 us (49%)
  Pallas kernels  21 us (24%)
  starting transfers between devices  12.1 us (14%)
  local copies, waits for them, and re-layouts  6.8 us (8%)
  waiting for transfers between devices  3.52 us (4%)
    all_to_all x3, blocking collectives, exchanged(): return lax.all_to_all(value, AXES, 0, 0, axis_index_groups=groups)  42.9 us
    pallas_call x2, Pallas kernels, attend(): pl.pallas_call(functools.partial(attend_kernel, far, chained), grid_spec=...  14.5 us
    ppermute x2, starting transfers between devices, swapped(): return lax.ppermute(value, AXES, [(i, i ^ bit) for i in range(count)])  6.91 us
    unnamed x24, local copies, waits for them, and re-layouts  6.72 us
    ppermute x2, starting transfers between devices, shifted(): lax.ppermute(value, axis, [(i, (i + by) % devices) for i in range(devices)])  5.21 us
    pallas_call x1, Pallas kernels, latents(): pl.pallas_call(functools.partial(latent_kernel, steps), grid_spec=pltpu.P...  3 us
    pallas_call x2, Pallas kernels, outer(): pl.pallas_call(functools.partial(outer_kernel, fresh is not None), grid_s...  2.39 us
    ppermute x2, waiting for transfers between devices, shifted(): lax.ppermute(value, axis, [(i, (i + by) % devices) for i in range(devices)])  1.97 us
  transfers between devices with their start and end apart: 4, of which 3 were waited for; matrix products, arithmetic and copies ran while one was open for 0% of the time, Pallas kernels for 8%

commit v1 on v0

--- a/solution.py
+++ b/solution.py
@@ -18,7 +18,7 @@
 AXES = ("seq", "dp")
 CORE_BIT = 16
 PLANE_BITS = (32, 64, 128, 8)
-DEPTH_BITS = (1, 2, 4)
+DEPTH_STEPS = (1, 2, 7)
 CHUNKS = 32
 CHUNK_ROWS = 96
 NT = (((1,), (1,)), ((), ()))
@@ -72,72 +72,82 @@
     return jnp.dot(a, b, preferred_element_type=F32)
 
 
-def latent_kernel(steps, place_ref, x_ref, dq_ref, dv_ref, k_ref, vf_ref, upv_ref, lat_ref, latt_ref, value_ref, send_ref, acc):
-    step = pl.program_id(0)
-    down = jnp.concatenate([dq_ref[...], dv_ref[...]], axis=0)
-    part = dot_nt(x_ref[...], down)
-
-    @pl.when(step == 0)
-    def _():
-        acc[...] = part
-
-    @pl.when(step > 0)
-    def _():
-        acc[...] += part
-
-    @pl.when(step == steps - 1)
-    def _():
-        whole = acc[...]
-        lat = whole.astype(BF16)
-        lat_ref[...] = lat
-        latt_ref[...] = whole.T.astype(BF16)
-        up = dot(lat[:, RANK:], upv_ref[...])
-        value_ref[...] = (vf_ref[...].astype(F32) + adapter_scale * up).astype(BF16)
-        half = value_ref.shape[1] // 2
-        sent = pl.ds(pl.multiple_of(place_ref[0] * half, half), half)
-        send_ref[:, :half] = k_ref[:, sent]
-        send_ref[:, half:] = value_ref[:, sent]
-
-
-def latents(place, x, down_q, down_v, keys, value_frozen, up_v, steps=8):
+def in_hbm(value):
+    return pltpu.with_memory_space_constraint(value, pltpu.HBM)
+
+
+def latent_kernel(steps, place_ref, x_hbm, dq_hbm, dv_hbm, vf_hbm, upv_hbm, lat_ref, latt_ref, value_ref, send_ref, x_buf, down, vf_buf, up_buf, sems):
+    tokens, model = x_buf.shape
+    block = model // steps
+    first = [
+        pltpu.make_async_copy(dq_hbm, down.at[pl.ds(0, RANK)], sems.at[steps]),
+        pltpu.make_async_copy(dv_hbm, down.at[pl.ds(RANK, RANK)], sems.at[steps + 1]),
+    ]
+    last = [
+        pltpu.make_async_copy(vf_hbm, vf_buf, sems.at[steps + 2]),
+        pltpu.make_async_copy(upv_hbm, up_buf, sems.at[steps + 3]),
+    ]
+    pieces = []
+    for step in range(steps):
+        cols = pl.ds(step * block, block)
+        pieces.append(pltpu.make_async_copy(x_hbm.at[:, cols], x_buf.at[:, cols], sems.at[step]))
+    for copy in first + pieces + last:
+        copy.start()
+    for copy in first:
+        copy.wait()
+    whole = None
+    for step in range(steps):
+        pieces[step].wait()
+        cols = slice(step * block, (step + 1) * block)
+        part = dot_nt(x_buf[:, cols], down[:, cols])
+        whole = part if whole is None else whole + part
+    for copy in last:
+        copy.wait()
+    lat = whole.astype(BF16)
+    lat_ref[...] = lat
+    latt_ref[...] = whole.T.astype(BF16)
+    up = dot(lat[:, RANK:], up_buf[...])
+    value_ref[...] = (vf_buf[...].astype(F32) + adapter_scale * up).astype(BF16)
+    half = value_ref.shape[1] // 2
+    send_ref[...] = value_ref[:, pl.ds(pl.multiple_of(place_ref[0] * half, half), half)]
+
+
+def latents(place, x, down_q, down_v, value_frozen, up_v, steps=8):
     tokens, model = x.shape
-    block = model // steps
     cols = value_frozen.shape[1]
-    along = lambda i, s: (0, i)
     whole = lambda i, s: (0, 0)
     return pl.pallas_call(
         functools.partial(latent_kernel, steps),
         grid_spec=pltpu.PrefetchScalarGridSpec(
             num_scalar_prefetch=1,
-            grid=(steps,),
-            in_specs=[
-                pl.BlockSpec((tokens, block), along),
-                pl.BlockSpec((RANK, block), along),
-                pl.BlockSpec((RANK, block), along),
-                pl.BlockSpec((tokens, cols), whole),
-                pl.BlockSpec((tokens, cols), whole),
-                pl.BlockSpec((RANK, cols), whole),
-            ],
+            grid=(1,),
+            in_specs=[pl.BlockSpec(memory_space=pl.ANY)] * 5,
             out_specs=[
                 pl.BlockSpec((tokens, 2 * RANK), whole),
                 pl.BlockSpec((2 * RANK, tokens), whole),
                 pl.BlockSpec((tokens, cols), whole),
-                pl.BlockSpec((tokens, cols), whole),
+                pl.BlockSpec((tokens, cols // 2), whole),
             ],
-            scratch_shapes=[pltpu.VMEM((tokens, 2 * RANK), F32)],
+            scratch_shapes=[
+                pltpu.VMEM((tokens, model), BF16),
+                pltpu.VMEM((2 * RANK, model), BF16),
+                pltpu.VMEM((tokens, cols), BF16),
+                pltpu.VMEM((RANK, cols), BF16),
+                pltpu.SemaphoreType.DMA((steps + 4,)),
+            ],
         ),
         out_shape=[
             jax.ShapeDtypeStruct((tokens, 2 * RANK), BF16),
             jax.ShapeDtypeStruct((2 * RANK, tokens), BF16),
             jax.ShapeDtypeStruct((tokens, cols), BF16),
-            jax.ShapeDtypeStruct((tokens, cols), BF16),
+            jax.ShapeDtypeStruct((tokens, cols // 2), BF16),
         ],
-        compiler_params=pltpu.CompilerParams(vmem_limit_bytes=VMEM_LIMIT),
+        compiler_params=pltpu.CompilerParams(vmem_limit_bytes=48 * 1024 * 1024),
         cost_estimate=pl.CostEstimate(
             flops=2 * tokens * model * 2 * RANK, bytes_accessed=2 * tokens * model, transcendentals=0
         ),
         name="latents",
-    )(place, x, down_q, down_v, keys, value_frozen, up_v)
+    )(place, *[in_hbm(a) for a in (x, down_q, down_v, value_frozen, up_v)])
 
 
 def attend_kernel(far, chained, first_ref, *refs):
@@ -233,11 +243,8 @@
         pl.BlockSpec((tokens, WIDTH), at_group),
     ]
     if far:
-        args += [prev, prev]
-        specs += [
-            pl.BlockSpec((tokens, WIDTH), at_step),
-            pl.BlockSpec((tokens, WIDTH), lambda i, s: (0, groups + i)),
-        ]
+        args += list(prev)
+        specs += [pl.BlockSpec((tokens, WIDTH), at_group), pl.BlockSpec((tokens, WIDTH), at_step)]
     args += [lat, latt, up_q]
     specs += [
         pl.BlockSpec((tokens, 2 * RANK), whole),
@@ -420,7 +427,9 @@
 def summed(given, kept):
     halves = kept + swapped(given, CORE_BIT).astype(F32)
     piece = sum_over_first(exchanged(halves.astype(BF16), PLANE_BITS))
-    piece = sum_over_first(spread(piece.astype(BF16), DEPTH_BITS))
+    for bits in DEPTH_STEPS:
+        mine = piece.astype(BF16)
+        piece = mine.astype(F32) + swapped(mine, bits).astype(F32)
     return spread(piece.astype(BF16), PLANE_BITS)
 
 
@@ -443,10 +452,11 @@
     place = parity.reshape(1).astype(jnp.int32)
     away = 1 - place
     pair = KEY_VALUE_HEADS // 2
+    prev_keys = shifted(keys, "seq", 1)
     lat, latt, values, sent = latents(
-        place, x, query_down_weight.T, value_down_weight.T, keys, vf, value_up_weight
-    )
-    prev = shifted(sent, "seq", 1)
+        place, x, query_down_weight.T, value_down_weight.T, vf, value_up_weight
+    )
+    prev = (prev_keys, shifted(sent, "seq", 1))
     out, bq, upt, dv_near = attend(
         pair * place, pair, qf, dout, keys, values, None, lat, latt, query_up_weight, None
     )

time: 87.6 us -> 80.4 us (0.918)
  blocking collectives: 42.9 us -> 26.3 us
  starting transfers between devices: 12.1 us -> 22.1 us
  local copies, waits for them, and re-layouts: 6.8 us -> 0.08 us
  waiting for transfers between devices: 3.52 us -> 8.54 us
  Pallas kernels: 21 us -> 22.3 us
    all_to_all x3 -> x2, blocking collectives: 42.9 us -> 26.3 us  [exchanged(): return lax.all_to_all(value, AXES, 0, 0, axis_index_groups=groups)]
    ppermute x2 -> x5, starting transfers between devices: 6.91 us -> 18.1 us  [swapped(): return lax.ppermute(value, AXES, [(i, i ^ bit) for i in range(count)])]
    unnamed x24 -> x12, local copies, waits for them, and re-layouts: 6.72 us -> 0.02 us
    ppermute x2 -> x5, waiting for transfers between devices: 1.55 us -> 5.2 us  [swapped(): return lax.ppermute(value, AXES, [(i, i ^ bit) for i in range(count)])]
    ppermute x2 -> x3, waiting for transfers between devices: 1.97 us -> 3.34 us  [shifted(): lax.ppermute(value, axis, [(i, (i + by) % devices) for i in range(devices)])]
    pallas_call x1, Pallas kernels: 3 us -> 4.32 us  [latents(): pl.pallas_call(functools.partial(latent_kernel, steps), grid_spec=pltpu.P...]
    ppermute x2 -> x3, starting transfers between devices: 5.21 us -> 3.96 us  [shifted(): lax.ppermute(value, axis, [(i, (i + by) % devices) for i in range(devices)])]
  transfers between devices with their start and end apart: 4 -> 8, of which waited for: 3 -> 6; matrix products, arithmetic and copies ran while one was open for 0% -> 0% of each run, Pallas kernels for 8% -> 14%
where the time goes in v1:
time: 80.4 us; the launch traced here: 80.3 us
  blocking collectives  26.3 us (33%)
  Pallas kernels  22.3 us (28%)
  starting transfers between devices  22.1 us (27%)
  waiting for transfers between devices  8.54 us (11%)
    all_to_all x2, blocking collectives, exchanged(): return lax.all_to_all(value, AXES, 0, 0, axis_index_groups=groups)  26.3 us
    ppermute x5, starting transfers between devices, swapped(): return lax.ppermute(value, AXES, [(i, i ^ bit) for i in range(count)])  18.1 us
    pallas_call x2, Pallas kernels, attend(): pl.pallas_call(functools.partial(attend_kernel, far, chained), grid_spec=...  14.5 us
    ppermute x5, waiting for transfers between devices, swapped(): return lax.ppermute(value, AXES, [(i, i ^ bit) for i in range(count)])  5.2 us
    pallas_call x1, Pallas kernels, latents(): pl.pallas_call(functools.partial(latent_kernel, steps), grid_spec=pltpu.P...  4.32 us
    ppermute x3, starting transfers between devices, shifted(): lax.ppermute(value, axis, [(i, (i + by) % devices) for i in range(devices)])  3.96 us
    ppermute x3, waiting for transfers between devices, shifted(): lax.ppermute(value, axis, [(i, (i + by) % devices) for i in range(devices)])  3.34 us
    pallas_call x2, Pallas kernels, outer(): pl.pallas_call(functools.partial(outer_kernel, fresh is not None), grid_s...  2.39 us
  transfers between devices with their start and end apart: 8, of which 6 were waited for; matrix products, arithmetic and copies ran while one was open for 0% of the time, Pallas kernels for 14%

profile of v1, /device:TPU:1, one launch (start us, length us, event | category | flops | bytes accessed | tf_op | source)
XLA Modules:
  0.0 80.3 jit_solution(13666360573025534952)
XLA Ops:
  0.6 2.8 %collective-permute-start = (bf16[256,512]{1,0:T(8,128)(2,1)}, bf16[256,512]{1,0:T(8,128)(2,1)S(1)}, u32[]{:S(2)}, u32[]{:S(2)}) collective-permute-start(bf16[256,512]{1,0:T(8,128)(2,1)} %bitcast.18), channel_id=1, source_target_pairs={{0,16},{16,32},{32,48},{48,64},{64,80},{80,96},{96,112},{112,128},... | collective-permute-start | bytes 786440 | tf_op jit(solution)/shard_map/ppermute | solution.py:64
  3.4 4.3 %latents.1 = (bf16[256,32]{1,0:T(8,128)(2,1)S(1)}, bf16[32,256]{1,0:T(8,128)(2,1)S(1)}, bf16[256,512]{1,0:T(8,128)(2,1)S(1)}, bf16[256,256]{1,0:T(8,128)(2,1)S(1)}) custom-call(s32[1]{0:T(128)} %bitcast.place_ref.half_ref, bf16[256,8192]{1,0:T(8,128)(2,1)} %bitcast.11, bf16[16,8192]{1,0:T(8,128)(2,1)} %bitcast.21, bf16[16,8192]{1,0:T(8,128)(2,1)} %bitcast.22, ...), custom_call_target="tpu_custom_call" | custom-call | flops 134217728 | bytes 4194304 | tf_op jit(solution)/shard_map/latents/pallas_call | solution.py:119
  7.7 0.1 collective-permute-start.1
  7.9 6.0 %attend_near.1 = (bf16[256,4096]{1,0:T(8,128)(2,1)}, f32[16,4096]{1,0:T(8,128)S(1)}, f32[16,256]{1,0:T(8,128)S(1)}, f32[256,256]{1,0:T(8,128)S(1)}) custom-call(s32[1]{0:T(128)S(6)} %mul.7.first_ref, bf16[256,4096]{1,0:T(8,128)(2,1)S(1)} %bitcast.14, bf16[256,4096]{1,0:T(8,128)(2,1)S(1)} %bitcast.16, bf16[256,512]{1,0:T(8,128)(2,1)S(1)} %bitcast.19, ...), custom_call_target="tpu_custom_call" | custom-call | flops 1342177280 | bytes 3145728 | tf_op jit(solution)/shard_map/attend_near/pallas_call | solution.py:275
  13.9 8.6 %attend_far.1 = (bf16[256,4096]{1,0:T(8,128)(2,1)}, f32[16,4096]{1,0:T(8,128)S(1)}, f32[16,256]{1,0:T(8,128)S(1)}, f32[256,256]{1,0:T(8,128)S(1)}, bf16[256,256]{1,0:T(8,128)(2,1)S(1)}) custom-call(s32[1]{0:T(128)S(6)} %mul.6.first_ref, bf16[256,4096]{1,0:T(8,128)(2,1)S(1)} %bitcast.15, ...), custom_call_target="tpu_custom_call", output_to_operand_aliasing={{0}: (10, {}), {1}: (11, {})} | custom-call | flops 2684354560 | bytes 3145728 | tf_op jit(solution)/shard_map/attend_far/pallas_call | solution.py:275
  22.4 1.1 %collective-permute-start.2 = (bf16[256,256]{1,0:T(8,128)(2,1)S(1)}, bf16[256,256]{1,0:T(8,128)(2,1)S(1)}, u32[]{:S(2)}, u32[]{:S(2)}) collective-permute-start(bf16[256,256]{1,0:T(8,128)(2,1)S(1)} %get-tuple-element.37), channel_id=1, source_target_pairs={{0,240},{16,0},{32,16},{48,32},{64,48},{80,64},{96,80},{112,96},{1... | collective-permute-start | bytes 393224 | tf_op jit(solution)/shard_map/ppermute | solution.py:64
  23.5 3.3 %collective-permute-done.2.refs_6_ = bf16[256,256]{1,0:T(8,128)(2,1)S(1)} collective-permute-done((bf16[256,256]{1,0:T(8,128)(2,1)S(1)}, bf16[256,256]{1,0:T(8,128)(2,1)S(1)}, u32[]{:S(2)}, u32[]{:S(2)}) %collective-permute-start.2) | collective-permute-done | bytes 131104 | tf_op jit(solution)/shard_map/ppermute | solution.py:64
  26.8 1.2 %outer_first.1 = (bf16[16,96,128]{2,1,0:T(8,128)(2,1)S(1)}, bf16[32,256]{1,0:T(8,128)(2,1)S(1)}, bf16[256,256]{1,0:T(8,128)(2,1)S(1)}) custom-call(s32[1]{0:T(128)S(6)} %sub.3.half_ref, bf16[256,8192]{1,0:T(8,128)(2,1)S(1)} %bitcast.12, f32[16,4096]{1,0:T(8,128)S(1)} %get-tuple-element.33.refs_1_, ...), custom_call_target="tpu_custom_call" | custom-call | flops 67108864 | bytes 2097152 | tf_op jit(solution)/shard_map/outer_first/pallas_call | solution.py:368
  28.1 2.6 %collective-permute-start.3 = (bf16[16,96,128]{2,1,0:T(8,128)(2,1)S(1)}, bf16[16,96,128]{2,1,0:T(8,128)(2,1)S(1)}, u32[]{:S(2)}, u32[]{:S(2)}) collective-permute-start(bf16[16,96,128]{2,1,0:T(8,128)(2,1)S(1)} %get-tuple-element.40), channel_id=1, source_target_pairs={{0,16},{1,17},{2,18},{3,19},{4,20},{5,21},{6,22},{7,23},{8,24},{9,... | collective-permute-start | bytes 1179656 | tf_op jit(solution)/shard_map/ppermute | solution.py:59
  30.7 1.1 %outer_second.1 = f32[16,96,128]{2,1,0:T(8,128)S(1)} custom-call(s32[1]{0:T(128)} %bitcast.place_ref.half_ref, bf16[256,8192]{1,0:T(8,128)(2,1)S(1)} %bitcast.13, f32[16,4096]{1,0:T(8,128)S(1)} %get-tuple-element.33.refs_1_, bf16[32,256]{1,0:T(8,128)(2,1)S(1)} %get-tuple-element.28.refs_5_.refs_7_.refs_2_, bf16[256,256]{1,0:T(8,128)(2,1)S(1)} %get-tuple-element.38.refs_3_, ...), custom_call_target="tpu_custom_call" | custom-call | flops 67108864 | bytes 2097152 | tf_op jit(solution)/shard_map/outer_second/pallas_call | solution.py:368
  31.9 0.2 collective-permute-done.3
  32.1 0.1 add_convert_fusion
  32.2 14.9 %all_to_all.10 = bf16[16,96,128]{2,1,0:T(8,128)(2,1)S(1)} all-to-all(bf16[16,96,128]{2,1,0:T(8,128)(2,1)S(1)} %add_convert_fusion), channel_id=1, replica_groups={{0,32,64,96,128,160,192,224,8,40,72,104,136,168,200,232},{1,33,65,97,12..., dimensions={0} | all-to-all | bytes 786432 | tf_op jit(solution)/shard_map/all_to_all | solution.py:45
  47.1 0.1 reduce_sum.12
  47.1 1.7 %collective-permute-start.4 = (bf16[96,128]{1,0:T(8,128)(2,1)S(1)}, bf16[96,128]{1,0:T(8,128)(2,1)S(1)}, u32[]{:S(2)}, u32[]{:S(2)}) collective-permute-start(bf16[96,128]{1,0:T(8,128)(2,1)S(1)} %reduce_sum.12), channel_id=1, source_target_pairs={{0,1},{1,0},{2,3},{3,2},{4,5},{5,4},{6,7},{7,6},{8,9},{9,8},{10,11... | collective-permute-start | bytes 73736 | tf_op jit(solution)/shard_map/ppermute | solution.py:59
  48.8 1.2 %collective-permute-done.4 = bf16[96,128]{1,0:T(8,128)(2,1)S(1)} collective-permute-done((bf16[96,128]{1,0:T(8,128)(2,1)S(1)}, bf16[96,128]{1,0:T(8,128)(2,1)S(1)}, u32[]{:S(2)}, u32[]{:S(2)}) %collective-permute-start.4) | collective-permute-done | bytes 24608 | tf_op jit(solution)/shard_map/ppermute | solution.py:59
  50.1 3.1 %collective-permute-start.5 = (bf16[96,128]{1,0:T(8,128)(2,1)S(1)}, bf16[96,128]{1,0:T(8,128)(2,1)S(1)}, u32[]{:S(2)}, u32[]{:S(2)}) collective-permute-start(bf16[96,128]{1,0:T(8,128)(2,1)S(1)} %add_convert_fusion.3), channel_id=1, source_target_pairs={{0,2},{1,3},{2,0},{3,1},{4,6},{5,7},{6,4},{7,5},{8,10},{9,11},{10,... | collective-permute-start | bytes 73736 | tf_op jit(solution)/shard_map/ppermute | solution.py:59
  53.1 1.2 %collective-permute-done.5 = bf16[96,128]{1,0:T(8,128)(2,1)S(1)} collective-permute-done((bf16[96,128]{1,0:T(8,128)(2,1)S(1)}, bf16[96,128]{1,0:T(8,128)(2,1)S(1)}, u32[]{:S(2)}, u32[]{:S(2)}) %collective-permute-start.5) | collective-permute-done | bytes 24608 | tf_op jit(solution)/shard_map/ppermute | solution.py:59
  54.4 4.9 %collective-permute-start.6 = (bf16[96,128]{1,0:T(8,128)(2,1)S(1)}, bf16[96,128]{1,0:T(8,128)(2,1)S(1)}, u32[]{:S(2)}, u32[]{:S(2)}) collective-permute-start(bf16[96,128]{1,0:T(8,128)(2,1)S(1)} %add_convert_fusion.2), channel_id=1, source_target_pairs={{0,7},{1,6},{2,5},{3,4},{4,3},{5,2},{6,1},{7,0},{8,15},{9,14},{10,... | collective-permute-start | bytes 73736 | tf_op jit(solution)/shard_map/ppermute | solution.py:59
  59.2 1.2 %collective-permute-done.6 = bf16[96,128]{1,0:T(8,128)(2,1)S(1)} collective-permute-done((bf16[96,128]{1,0:T(8,128)(2,1)S(1)}, bf16[96,128]{1,0:T(8,128)(2,1)S(1)}, u32[]{:S(2)}, u32[]{:S(2)}) %collective-permute-start.6) | collective-permute-done | bytes 24608 | tf_op jit(solution)/shard_map/ppermute | solution.py:59
  60.5 11.4 %all_to_all.11.own_ref = bf16[16,96,128]{2,1,0:T(8,128)(2,1)S(1)} all-to-all(bf16[16,96,128]{2,1,0:T(8,128)(2,1)S(1)} %broadcast_in_dim.10), channel_id=1, replica_groups={{0,32,64,96,128,160,192,224,8,40,72,104,136,168,200,232},{1,33,65,97,12..., dimensions={0} | all-to-all | bytes 786432 | tf_op jit(solution)/shard_map/all_to_all | solution.py:45
  71.9 5.9 %collective-permute-start.7 = (bf16[16,96,128]{2,1,0:T(8,128)(2,1)S(1)}, bf16[16,96,128]{2,1,0:T(8,128)(2,1)S(1)}, u32[]{:S(2)}, u32[]{:S(2)}) collective-permute-start(bf16[16,96,128]{2,1,0:T(8,128)(2,1)S(1)} %all_to_all.11.own_ref), channel_id=1, source_target_pairs={{0,16},{1,17},{2,18},{3,19},{4,20},{5,21},{6,22},{7,23},{8,24},{9,... | collective-permute-start | bytes 1179656 | tf_op jit(solution)/shard_map/ppermute | solution.py:59
  77.8 1.3 %collective-permute-done.7.other_ref = bf16[16,96,128]{2,1,0:T(8,128)(2,1)S(1)} collective-permute-done((bf16[16,96,128]{2,1,0:T(8,128)(2,1)S(1)}, bf16[16,96,128]{2,1,0:T(8,128)(2,1)S(1)}, u32[]{:S(2)}, u32[]{:S(2)}) %collective-permute-start.7) | collective-permute-done | bytes 393248 | tf_op jit(solution)/shard_map/ppermute | solution.py:59
  79.2 1.1 %unpack.1 = (f32[16,8192]{1,0:T(8,128)}, f32[16,8192]{1,0:T(8,128)}, f32[16,4096]{1,0:T(8,128)}, f32[16,512]{1,0:T(8,128)}) custom-call(s32[1]{0:T(128)} %bitcast.place_ref.half_ref, bf16[16,96,128]{2,1,0:T(8,128)(2,1)S(1)} %all_to_all.11.own_ref, bf16[16,96,128]{2,1,0:T(8,128)(2,1)S(1)} %collective-permute-done.7.other_ref), custom_call_target="tpu_custom_call" | custom-call | bytes 3145728 | tf_op jit(solution)/shard_map/unpack/pallas_call | solution.py:412
  (18 shorter events, 0.1 us)
Async XLA Ops:
  0.6 13.2 %collective-permute-start = (bf16[256,512]{1,0:T(8,128)(2,1)}, bf16[256,512]{1,0:T(8,128)(2,1)S(1)}, u32[]{:S(2)}, u32[]{:S(2)}) collective-permute-start(bf16[256,512]{1,0:T(8,128)(2,1)} %bitcast.18), channel_id=1, source_target_pairs={{0,16},{16,32},{32,48},{48,64},{64,80},{80,96},{96,112},{112,128},... | collective-permute-start | bytes 786440 | tf_op jit(solution)/shard_map/ppermute | solution.py:64
  3.4 4.5 %copy-start.2 = (bf16[1,256,4096]{2,1,0:T(8,128)(2,1)S(1)}, bf16[1,256,4096]{2,1,0:T(8,128)(2,1)}, u32[]{:S(2)}) copy-start(bf16[1,256,4096]{2,1,0:T(8,128)(2,1)} %param.10) | copy-start | bytes 6291460
  3.4 4.5 %copy-start.3 = (bf16[1,256,4096]{2,1,0:T(8,128)(2,1)S(1)}, bf16[1,256,4096]{2,1,0:T(8,128)(2,1)}, u32[]{:S(2)}) copy-start(bf16[1,256,4096]{2,1,0:T(8,128)(2,1)} %param.17) | copy-start | bytes 6291460
  3.4 4.5 %copy-start.4 = (bf16[1,256,512]{2,1,0:T(8,128)(2,1)S(1)}, bf16[1,256,512]{2,1,0:T(8,128)(2,1)}, u32[]{:S(2)}) copy-start(bf16[1,256,512]{2,1,0:T(8,128)(2,1)} %param.11) | copy-start | bytes 786436
  3.4 4.5 %copy-start.5 = (bf16[16,4096]{1,0:T(8,128)(2,1)S(1)}, bf16[16,4096]{1,0:T(8,128)(2,1)}, u32[]{:S(2)}) copy-start(bf16[16,4096]{1,0:T(8,128)(2,1)} %refs_8_.2) | copy-start | bytes 393220
  7.7 6.1 %collective-permute-start.1 = (bf16[256,256]{1,0:T(8,128)(2,1)S(1)}, bf16[256,256]{1,0:T(8,128)(2,1)S(1)}, u32[]{:S(2)}, u32[]{:S(2)}) collective-permute-start(bf16[256,256]{1,0:T(8,128)(2,1)S(1)} %get-tuple-element.26), channel_id=1, source_target_pairs={{0,16},{16,32},{32,48},{48,64},{64,80},{80,96},{96,112},{112,128},... | collective-permute-start | bytes 393224 | tf_op jit(solution)/shard_map/ppermute | solution.py:64
  13.8 13.0 %copy-start = (bf16[1,256,8192]{2,1,0:T(8,128)(2,1)S(1)}, bf16[1,256,8192]{2,1,0:T(8,128)(2,1)}, u32[]{:S(2)}) copy-start(bf16[1,256,8192]{2,1,0:T(8,128)(2,1)} %param.9) | copy-start | bytes 12582916
  13.9 13.0 %copy-start.1 = (bf16[16,512]{1,0:T(8,128)(2,1)S(1)}, bf16[16,512]{1,0:T(8,128)(2,1)}, u32[]{:S(2)}) copy-start(bf16[16,512]{1,0:T(8,128)(2,1)} %refs_8_.3) | copy-start | bytes 49156
  22.4 4.4 %collective-permute-start.2 = (bf16[256,256]{1,0:T(8,128)(2,1)S(1)}, bf16[256,256]{1,0:T(8,128)(2,1)S(1)}, u32[]{:S(2)}, u32[]{:S(2)}) collective-permute-start(bf16[256,256]{1,0:T(8,128)(2,1)S(1)} %get-tuple-element.37), channel_id=1, source_target_pairs={{0,240},{16,0},{32,16},{48,32},{64,48},{80,64},{96,80},{112,96},{1... | collective-permute-start | bytes 393224 | tf_op jit(solution)/shard_map/ppermute | solution.py:64
  28.1 4.0 %collective-permute-start.3 = (bf16[16,96,128]{2,1,0:T(8,128)(2,1)S(1)}, bf16[16,96,128]{2,1,0:T(8,128)(2,1)S(1)}, u32[]{:S(2)}, u32[]{:S(2)}) collective-permute-start(bf16[16,96,128]{2,1,0:T(8,128)(2,1)S(1)} %get-tuple-element.40), channel_id=1, source_target_pairs={{0,16},{1,17},{2,18},{3,19},{4,20},{5,21},{6,22},{7,23},{8,24},{9,... | collective-permute-start | bytes 1179656 | tf_op jit(solution)/shard_map/ppermute | solution.py:59
  47.1 2.9 %collective-permute-start.4 = (bf16[96,128]{1,0:T(8,128)(2,1)S(1)}, bf16[96,128]{1,0:T(8,128)(2,1)S(1)}, u32[]{:S(2)}, u32[]{:S(2)}) collective-permute-start(bf16[96,128]{1,0:T(8,128)(2,1)S(1)} %reduce_sum.12), channel_id=1, source_target_pairs={{0,1},{1,0},{2,3},{3,2},{4,5},{5,4},{6,7},{7,6},{8,9},{9,8},{10,11... | collective-permute-start | bytes 73736 | tf_op jit(solution)/shard_map/ppermute | solution.py:59
  50.1 4.3 %collective-permute-start.5 = (bf16[96,128]{1,0:T(8,128)(2,1)S(1)}, bf16[96,128]{1,0:T(8,128)(2,1)S(1)}, u32[]{:S(2)}, u32[]{:S(2)}) collective-permute-start(bf16[96,128]{1,0:T(8,128)(2,1)S(1)} %add_convert_fusion.3), channel_id=1, source_target_pairs={{0,2},{1,3},{2,0},{3,1},{4,6},{5,7},{6,4},{7,5},{8,10},{9,11},{10,... | collective-permute-start | bytes 73736 | tf_op jit(solution)/shard_map/ppermute | solution.py:59
  54.4 6.1 %collective-permute-start.6 = (bf16[96,128]{1,0:T(8,128)(2,1)S(1)}, bf16[96,128]{1,0:T(8,128)(2,1)S(1)}, u32[]{:S(2)}, u32[]{:S(2)}) collective-permute-start(bf16[96,128]{1,0:T(8,128)(2,1)S(1)} %add_convert_fusion.2), channel_id=1, source_target_pairs={{0,7},{1,6},{2,5},{3,4},{4,3},{5,2},{6,1},{7,0},{8,15},{9,14},{10,... | collective-permute-start | bytes 73736 | tf_op jit(solution)/shard_map/ppermute | solution.py:59
  71.9 7.2 %collective-permute-start.7 = (bf16[16,96,128]{2,1,0:T(8,128)(2,1)S(1)}, bf16[16,96,128]{2,1,0:T(8,128)(2,1)S(1)}, u32[]{:S(2)}, u32[]{:S(2)}) collective-permute-start(bf16[16,96,128]{2,1,0:T(8,128)(2,1)S(1)} %all_to_all.11.own_ref), channel_id=1, source_target_pairs={{0,16},{1,17},{2,18},{3,19},{4,20},{5,21},{6,22},{7,23},{8,24},{9,... | collective-permute-start | bytes 1179656 | tf_op jit(solution)/shard_map/ppermute | solution.py:59

commit v2 on v1

--- a/solution.py
+++ b/solution.py
@@ -17,7 +17,7 @@
 masked_score = -1e30
 AXES = ("seq", "dp")
 CORE_BIT = 16
-PLANE_BITS = (32, 64, 128, 8)
+PLANE_BITS = (128, 8, 32, 64)
 DEPTH_STEPS = (1, 2, 7)
 CHUNKS = 32
 CHUNK_ROWS = 96
@@ -198,9 +198,13 @@
         expo = jnp.exp2((score - top) * base2)
         prob = expo * (1.0 / jnp.sum(expo, axis=1, keepdims=True))
         prob_b = prob.astype(BF16)
-        attended = dot(prob_b, values)
+        if far:
+            attended = dot(prob_b, values)
+            dprob = dot_nt(do, values)
+        else:
+            dprob = dot_nt(do, values)
+            attended = dot(prob_b, values)
         delta = jnp.sum(do.astype(F32) * attended, axis=1, keepdims=True)
-        dprob = dot_nt(do, values)
         dscore = (prob * (dprob - delta)).astype(BF16)
         dq_rows = (dot(dscore, keys) * root).astype(BF16)
         for n, cols in enumerate(slices):
@@ -383,45 +387,38 @@
     )(half, *args)
 
 
-def unpack_kernel(scale, half_ref, own_ref, other_ref, aq_ref, av_ref, bq_ref, bv_ref):
-    def fill(ref):
-        for chunk in range(CHUNKS // 2):
-            for lane in range(2):
-                cols = slice((2 * chunk + lane) * WIDTH, (2 * chunk + lane + 1) * WIDTH)
-                rows = slice(lane * RANK, (lane + 1) * RANK)
-                aq_ref[:, cols] = ref[chunk, rows, :].astype(F32) * scale
-                rows = slice((2 + lane) * RANK, (3 + lane) * RANK)
-                av_ref[:, cols] = ref[chunk, rows, :].astype(F32) * scale
-            cols = slice(chunk * WIDTH, (chunk + 1) * WIDTH)
-            bq_ref[:, cols] = ref[chunk, 4 * RANK : 5 * RANK, :].astype(F32) * scale
-            if chunk < 2:
-                bv_ref[:, cols] = ref[chunk, 5 * RANK :, :].astype(F32) * scale
-
-    @pl.when(pl.program_id(0) == 0)
-    def _():
-        fill(own_ref)
-
-    @pl.when(pl.program_id(0) == 1)
-    def _():
-        fill(other_ref)
-
-
-def unpacked(half, own, other, scale, shapes):
-    flip = lambda i, s: (0, (s[0] + i) % 2)
-    whole = lambda i, s: (0, 0, 0)
+def unpack_kernel(scale, half_ref, ref, *refs):
+    aq_ref, av_ref, bq_ref, bv_ref = refs[-4:]
+    for chunk in range(CHUNKS // 2):
+        for lane in range(2):
+            cols = slice((2 * chunk + lane) * WIDTH, (2 * chunk + lane + 1) * WIDTH)
+            rows = slice(lane * RANK, (lane + 1) * RANK)
+            aq_ref[:, cols] = ref[chunk, rows, :].astype(F32) * scale
+            rows = slice((2 + lane) * RANK, (3 + lane) * RANK)
+            av_ref[:, cols] = ref[chunk, rows, :].astype(F32) * scale
+        cols = slice(chunk * WIDTH, (chunk + 1) * WIDTH)
+        bq_ref[:, cols] = ref[chunk, 4 * RANK : 5 * RANK, :].astype(F32) * scale
+        if chunk < 2:
+            bv_ref[:, cols] = ref[chunk, 5 * RANK :, :].astype(F32) * scale
+
+
+def unpacked(half, chunks, scale, shapes, filled=()):
+    at_half = lambda i, s: (0, s[0])
     return pl.pallas_call(
         functools.partial(unpack_kernel, scale),
         grid_spec=pltpu.PrefetchScalarGridSpec(
             num_scalar_prefetch=1,
-            grid=(2,),
-            in_specs=[pl.BlockSpec(own.shape, whole)] * 2,
-            out_specs=[pl.BlockSpec((rows, cols // 2), flip) for rows, cols in shapes],
+            grid=(1,),
+            in_specs=[pl.BlockSpec(chunks.shape, lambda i, s: (0, 0, 0))]
+            + [pl.BlockSpec(memory_space=pl.ANY)] * len(filled),
+            out_specs=[pl.BlockSpec((rows, cols // 2), at_half) for rows, cols in shapes],
         ),
         out_shape=[jax.ShapeDtypeStruct(shape, F32) for shape in shapes],
+        input_output_aliases={2 + n: n for n in range(len(filled))},
         compiler_params=pltpu.CompilerParams(vmem_limit_bytes=VMEM_LIMIT),
-        cost_estimate=pl.CostEstimate(flops=0, bytes_accessed=3 * 1024 * 1024, transcendentals=0),
-        name="unpack",
-    )(half, own, other)
+        cost_estimate=pl.CostEstimate(flops=0, bytes_accessed=1024 * 1024, transcendentals=0),
+        name="unpack_other" if filled else "unpack_own",
+    )(half, chunks, *filled)
 
 
 def summed(given, kept):
@@ -473,7 +470,8 @@
     scale_factor = adapter_scale / math.sqrt(tokens * lax.axis_size("seq") * lax.axis_size("dp"))
     model = x.shape[1]
     shapes = [(RANK, model), (RANK, model), (RANK, qf.shape[1]), (RANK, vf.shape[1])]
-    aq, av, bq_sum, bv_sum = unpacked(place, own_half, other_half, scale_factor, shapes)
+    first_half = unpacked(place, own_half, scale_factor, shapes)
+    aq, av, bq_sum, bv_sum = unpacked(away, other_half, scale_factor, shapes, first_half)
     return (out[None], aq.T, bq_sum, av.T, bv_sum)
 
 

time: 80.4 us -> 79.7 us (level)
  waiting for transfers between devices: 8.54 us -> 7.24 us
    ppermute x5, waiting for transfers between devices: 5.2 us -> 4.35 us  [swapped(): return lax.ppermute(value, AXES, [(i, i ^ bit) for i in range(count)])]
    pallas_call x1 -> x2, Pallas kernels: 1.11 us -> 1.71 us  [unpacked(): pl.pallas_call(functools.partial(unpack_kernel, scale), grid_spec=pltpu.P...]
  transfers between devices with their start and end apart: 8 -> 8, of which waited for: 6 -> 6; matrix products, arithmetic and copies ran while one was open for 0% -> 0% of each run, Pallas kernels for 14% -> 15%
where the time goes in v2:
time: 79.7 us; the launch traced here: 79.5 us
  blocking collectives  26.5 us (33%)
  Pallas kernels  22.5 us (28%)
  starting transfers between devices  22.3 us (28%)
  waiting for transfers between devices  7.24 us (9%)
    all_to_all x2, blocking collectives, exchanged(): return lax.all_to_all(value, AXES, 0, 0, axis_index_groups=groups)  26.5 us
    ppermute x5, starting transfers between devices, swapped(): return lax.ppermute(value, AXES, [(i, i ^ bit) for i in range(count)])  17.9 us
    pallas_call x2, Pallas kernels, attend(): pl.pallas_call(functools.partial(attend_kernel, far, chained), grid_spec=...  14.1 us
    ppermute x3, starting transfers between devices, shifted(): lax.ppermute(value, axis, [(i, (i + by) % devices) for i in range(devices)])  4.4 us
    ppermute x5, waiting for transfers between devices, swapped(): return lax.ppermute(value, AXES, [(i, i ^ bit) for i in range(count)])  4.35 us
    pallas_call x1, Pallas kernels, latents(): pl.pallas_call(functools.partial(latent_kernel, steps), grid_spec=pltpu.P...  4.32 us
    ppermute x3, waiting for transfers between devices, shifted(): lax.ppermute(value, axis, [(i, (i + by) % devices) for i in range(devices)])  2.89 us
    pallas_call x2, Pallas kernels, outer(): pl.pallas_call(functools.partial(outer_kernel, fresh is not None), grid_s...  2.39 us
  transfers between devices with their start and end apart: 8, of which 6 were waited for; matrix products, arithmetic and copies ran while one was open for 0% of the time, Pallas kernels for 15%

profile of v2, /device:TPU:1, one launch (start us, length us, event | category | flops | bytes accessed | tf_op | source)
XLA Modules:
  0.0 79.5 jit_solution(13898830642199179132)
XLA Ops:
  0.6 2.8 %collective-permute-start = (bf16[256,512]{1,0:T(8,128)(2,1)}, bf16[256,512]{1,0:T(8,128)(2,1)S(1)}, u32[]{:S(2)}, u32[]{:S(2)}) collective-permute-start(bf16[256,512]{1,0:T(8,128)(2,1)} %bitcast.18), channel_id=1, source_target_pairs={{0,16},{16,32},{32,48},{48,64},{64,80},{80,96},{96,112},{112,128},... | collective-permute-start | bytes 786440 | tf_op jit(solution)/shard_map/ppermute | solution.py:64
  3.4 4.3 %latents.1 = (bf16[256,32]{1,0:T(8,128)(2,1)S(1)}, bf16[32,256]{1,0:T(8,128)(2,1)S(1)}, bf16[256,512]{1,0:T(8,128)(2,1)S(1)}, bf16[256,256]{1,0:T(8,128)(2,1)S(1)}) custom-call(s32[1]{0:T(128)} %bitcast.place_ref.half_ref, bf16[256,8192]{1,0:T(8,128)(2,1)} %bitcast.11, bf16[16,8192]{1,0:T(8,128)(2,1)} %bitcast.23, bf16[16,8192]{1,0:T(8,128)(2,1)} %bitcast.24, ...), custom_call_target="tpu_custom_call" | custom-call | flops 134217728 | bytes 4194304 | tf_op jit(solution)/shard_map/latents/pallas_call | solution.py:119
  7.7 0.1 collective-permute-start.1
  7.9 5.5 %attend_near.1 = (bf16[256,4096]{1,0:T(8,128)(2,1)}, f32[16,4096]{1,0:T(8,128)S(1)}, f32[16,256]{1,0:T(8,128)S(1)}, f32[256,256]{1,0:T(8,128)S(1)}) custom-call(s32[1]{0:T(128)S(6)} %mul.7.first_ref, bf16[256,4096]{1,0:T(8,128)(2,1)S(1)} %bitcast.14, bf16[256,4096]{1,0:T(8,128)(2,1)S(1)} %bitcast.16, bf16[256,512]{1,0:T(8,128)(2,1)S(1)} %bitcast.19, ...), custom_call_target="tpu_custom_call" | custom-call | flops 1342177280 | bytes 3145728 | tf_op jit(solution)/shard_map/attend_near/pallas_call | solution.py:279
  13.4 8.6 %attend_far.1 = (bf16[256,4096]{1,0:T(8,128)(2,1)}, f32[16,4096]{1,0:T(8,128)S(1)}, f32[16,256]{1,0:T(8,128)S(1)}, f32[256,256]{1,0:T(8,128)S(1)}, bf16[256,256]{1,0:T(8,128)(2,1)S(1)}) custom-call(s32[1]{0:T(128)S(6)} %mul.6.first_ref, bf16[256,4096]{1,0:T(8,128)(2,1)S(1)} %bitcast.15, ...), custom_call_target="tpu_custom_call", output_to_operand_aliasing={{0}: (10, {}), {1}: (11, {})} | custom-call | flops 2684354560 | bytes 3145728 | tf_op jit(solution)/shard_map/attend_far/pallas_call | solution.py:279
  22.0 1.5 %collective-permute-start.2 = (bf16[256,256]{1,0:T(8,128)(2,1)S(1)}, bf16[256,256]{1,0:T(8,128)(2,1)S(1)}, u32[]{:S(2)}, u32[]{:S(2)}) collective-permute-start(bf16[256,256]{1,0:T(8,128)(2,1)S(1)} %get-tuple-element.41), channel_id=1, source_target_pairs={{0,240},{16,0},{32,16},{48,32},{64,48},{80,64},{96,80},{112,96},{1... | collective-permute-start | bytes 393224 | tf_op jit(solution)/shard_map/ppermute | solution.py:64
  23.5 2.9 %collective-permute-done.2.refs_6_ = bf16[256,256]{1,0:T(8,128)(2,1)S(1)} collective-permute-done((bf16[256,256]{1,0:T(8,128)(2,1)S(1)}, bf16[256,256]{1,0:T(8,128)(2,1)S(1)}, u32[]{:S(2)}, u32[]{:S(2)}) %collective-permute-start.2) | collective-permute-done | bytes 131104 | tf_op jit(solution)/shard_map/ppermute | solution.py:64
  26.4 1.2 %outer_first.1 = (bf16[16,96,128]{2,1,0:T(8,128)(2,1)S(1)}, bf16[32,256]{1,0:T(8,128)(2,1)S(1)}, bf16[256,256]{1,0:T(8,128)(2,1)S(1)}) custom-call(s32[1]{0:T(128)S(6)} %sub.3.half_ref, bf16[256,8192]{1,0:T(8,128)(2,1)S(1)} %bitcast.12, f32[16,4096]{1,0:T(8,128)S(1)} %get-tuple-element.37.refs_1_, ...), custom_call_target="tpu_custom_call" | custom-call | flops 67108864 | bytes 2097152 | tf_op jit(solution)/shard_map/outer_first/pallas_call | solution.py:372
  27.6 2.6 %collective-permute-start.3 = (bf16[16,96,128]{2,1,0:T(8,128)(2,1)S(1)}, bf16[16,96,128]{2,1,0:T(8,128)(2,1)S(1)}, u32[]{:S(2)}, u32[]{:S(2)}) collective-permute-start(bf16[16,96,128]{2,1,0:T(8,128)(2,1)S(1)} %get-tuple-element.44), channel_id=1, source_target_pairs={{0,16},{1,17},{2,18},{3,19},{4,20},{5,21},{6,22},{7,23},{8,24},{9,... | collective-permute-start | bytes 1179656 | tf_op jit(solution)/shard_map/ppermute | solution.py:59
  30.3 1.1 %outer_second.1 = f32[16,96,128]{2,1,0:T(8,128)S(1)} custom-call(s32[1]{0:T(128)} %bitcast.place_ref.half_ref, bf16[256,8192]{1,0:T(8,128)(2,1)S(1)} %bitcast.13, f32[16,4096]{1,0:T(8,128)S(1)} %get-tuple-element.37.refs_1_, bf16[32,256]{1,0:T(8,128)(2,1)S(1)} %get-tuple-element.32.refs_5_.refs_7_.refs_2_, bf16[256,256]{1,0:T(8,128)(2,1)S(1)} %get-tuple-element.42.refs_3_, ...), custom_call_target="tpu_custom_call" | custom-call | flops 67108864 | bytes 2097152 | tf_op jit(solution)/shard_map/outer_second/pallas_call | solution.py:372
  31.4 0.2 collective-permute-done.3
  31.6 0.1 add_convert_fusion
  31.7 15.1 %all_to_all.10 = bf16[16,96,128]{2,1,0:T(8,128)(2,1)S(1)} all-to-all(bf16[16,96,128]{2,1,0:T(8,128)(2,1)S(1)} %add_convert_fusion), channel_id=1, replica_groups={{0,128,8,136,32,160,40,168,64,192,72,200,96,224,104,232},{1,129,9,137,3..., dimensions={0} | all-to-all | bytes 786432 | tf_op jit(solution)/shard_map/all_to_all | solution.py:45
  46.9 1.7 %collective-permute-start.4 = (bf16[96,128]{1,0:T(8,128)(2,1)S(1)}, bf16[96,128]{1,0:T(8,128)(2,1)S(1)}, u32[]{:S(2)}, u32[]{:S(2)}) collective-permute-start(bf16[96,128]{1,0:T(8,128)(2,1)S(1)} %reduce_sum.12), channel_id=1, source_target_pairs={{0,1},{1,0},{2,3},{3,2},{4,5},{5,4},{6,7},{7,6},{8,9},{9,8},{10,11... | collective-permute-start | bytes 73736 | tf_op jit(solution)/shard_map/ppermute | solution.py:59
  48.6 1.2 %collective-permute-done.4 = bf16[96,128]{1,0:T(8,128)(2,1)S(1)} collective-permute-done((bf16[96,128]{1,0:T(8,128)(2,1)S(1)}, bf16[96,128]{1,0:T(8,128)(2,1)S(1)}, u32[]{:S(2)}, u32[]{:S(2)}) %collective-permute-start.4) | collective-permute-done | bytes 24608 | tf_op jit(solution)/shard_map/ppermute | solution.py:59
  49.8 3.1 %collective-permute-start.5 = (bf16[96,128]{1,0:T(8,128)(2,1)S(1)}, bf16[96,128]{1,0:T(8,128)(2,1)S(1)}, u32[]{:S(2)}, u32[]{:S(2)}) collective-permute-start(bf16[96,128]{1,0:T(8,128)(2,1)S(1)} %add_convert_fusion.3), channel_id=1, source_target_pairs={{0,2},{1,3},{2,0},{3,1},{4,6},{5,7},{6,4},{7,5},{8,10},{9,11},{10,... | collective-permute-start | bytes 73736 | tf_op jit(solution)/shard_map/ppermute | solution.py:59
  52.9 1.2 %collective-permute-done.5 = bf16[96,128]{1,0:T(8,128)(2,1)S(1)} collective-permute-done((bf16[96,128]{1,0:T(8,128)(2,1)S(1)}, bf16[96,128]{1,0:T(8,128)(2,1)S(1)}, u32[]{:S(2)}, u32[]{:S(2)}) %collective-permute-start.5) | collective-permute-done | bytes 24608 | tf_op jit(solution)/shard_map/ppermute | solution.py:59
  54.1 4.9 %collective-permute-start.6 = (bf16[96,128]{1,0:T(8,128)(2,1)S(1)}, bf16[96,128]{1,0:T(8,128)(2,1)S(1)}, u32[]{:S(2)}, u32[]{:S(2)}) collective-permute-start(bf16[96,128]{1,0:T(8,128)(2,1)S(1)} %add_convert_fusion.2), channel_id=1, source_target_pairs={{0,7},{1,6},{2,5},{3,4},{4,3},{5,2},{6,1},{7,0},{8,15},{9,14},{10,... | collective-permute-start | bytes 73736 | tf_op jit(solution)/shard_map/ppermute | solution.py:59
  59.0 1.2 %collective-permute-done.6 = bf16[96,128]{1,0:T(8,128)(2,1)S(1)} collective-permute-done((bf16[96,128]{1,0:T(8,128)(2,1)S(1)}, bf16[96,128]{1,0:T(8,128)(2,1)S(1)}, u32[]{:S(2)}, u32[]{:S(2)}) %collective-permute-start.6) | collective-permute-done | bytes 24608 | tf_op jit(solution)/shard_map/ppermute | solution.py:59
  60.3 11.4 %all_to_all.11.ref = bf16[16,96,128]{2,1,0:T(8,128)(2,1)S(1)} all-to-all(bf16[16,96,128]{2,1,0:T(8,128)(2,1)S(1)} %broadcast_in_dim.10), channel_id=1, replica_groups={{0,128,8,136,32,160,40,168,64,192,72,200,96,224,104,232},{1,129,9,137,3..., dimensions={0} | all-to-all | bytes 786432 | tf_op jit(solution)/shard_map/all_to_all | solution.py:45
  71.7 5.6 %collective-permute-start.7 = (bf16[16,96,128]{2,1,0:T(8,128)(2,1)S(1)}, bf16[16,96,128]{2,1,0:T(8,128)(2,1)S(1)}, u32[]{:S(2)}, u32[]{:S(2)}) collective-permute-start(bf16[16,96,128]{2,1,0:T(8,128)(2,1)S(1)} %all_to_all.11.ref), channel_id=1, source_target_pairs={{0,16},{1,17},{2,18},{3,19},{4,20},{5,21},{6,22},{7,23},{8,24},{9,... | collective-permute-start | bytes 1179656 | tf_op jit(solution)/shard_map/ppermute | solution.py:59
  77.3 0.9 %unpack_own.1 = (f32[16,8192]{1,0:T(8,128)}, f32[16,8192]{1,0:T(8,128)}, f32[16,4096]{1,0:T(8,128)}, f32[16,512]{1,0:T(8,128)}) custom-call(s32[1]{0:T(128)} %bitcast.place_ref.half_ref, bf16[16,96,128]{2,1,0:T(8,128)(2,1)S(1)} %all_to_all.11.ref), custom_call_target="tpu_custom_call" | custom-call | bytes 1048576 | tf_op jit(solution)/shard_map/unpack_own/pallas_call | solution.py:407
  78.1 0.5 collective-permute-done.7.ref
  78.6 0.9 %unpack_other.1 = (f32[16,8192]{1,0:T(8,128)}, f32[16,8192]{1,0:T(8,128)}, f32[16,4096]{1,0:T(8,128)}, f32[16,512]{1,0:T(8,128)}) custom-call(s32[1]{0:T(128)S(6)} %sub.3.half_ref, bf16[16,96,128]{2,1,0:T(8,128)(2,1)S(1)} %collective-permute-done.7.ref, ...), custom_call_target="tpu_custom_call", output_to_operand_aliasing={{0}: (2, {}), {1}: (3, {}), {2}: (4, {}), {3}: (5, {})} | custom-call | bytes 1048576 | tf_op jit(solution)/shard_map/unpack_other/pallas_call | solution.py:407
  (19 shorter events, 0.2 us)
Async XLA Ops:
  0.6 12.8 %collective-permute-start = (bf16[256,512]{1,0:T(8,128)(2,1)}, bf16[256,512]{1,0:T(8,128)(2,1)S(1)}, u32[]{:S(2)}, u32[]{:S(2)}) collective-permute-start(bf16[256,512]{1,0:T(8,128)(2,1)} %bitcast.18), channel_id=1, source_target_pairs={{0,16},{16,32},{32,48},{48,64},{64,80},{80,96},{96,112},{112,128},... | collective-permute-start | bytes 786440 | tf_op jit(solution)/shard_map/ppermute | solution.py:64
  3.4 4.5 %copy-start.2 = (bf16[1,256,4096]{2,1,0:T(8,128)(2,1)S(1)}, bf16[1,256,4096]{2,1,0:T(8,128)(2,1)}, u32[]{:S(2)}) copy-start(bf16[1,256,4096]{2,1,0:T(8,128)(2,1)} %param.10) | copy-start | bytes 6291460
  3.4 4.5 %copy-start.3 = (bf16[1,256,4096]{2,1,0:T(8,128)(2,1)S(1)}, bf16[1,256,4096]{2,1,0:T(8,128)(2,1)}, u32[]{:S(2)}) copy-start(bf16[1,256,4096]{2,1,0:T(8,128)(2,1)} %param.17) | copy-start | bytes 6291460
  3.4 4.5 %copy-start.4 = (bf16[1,256,512]{2,1,0:T(8,128)(2,1)S(1)}, bf16[1,256,512]{2,1,0:T(8,128)(2,1)}, u32[]{:S(2)}) copy-start(bf16[1,256,512]{2,1,0:T(8,128)(2,1)} %param.11) | copy-start | bytes 786436
  3.4 4.5 %copy-start.5 = (bf16[16,4096]{1,0:T(8,128)(2,1)S(1)}, bf16[16,4096]{1,0:T(8,128)(2,1)}, u32[]{:S(2)}) copy-start(bf16[16,4096]{1,0:T(8,128)(2,1)} %refs_8_.2) | copy-start | bytes 393220
  7.7 5.7 %collective-permute-start.1 = (bf16[256,256]{1,0:T(8,128)(2,1)S(1)}, bf16[256,256]{1,0:T(8,128)(2,1)S(1)}, u32[]{:S(2)}, u32[]{:S(2)}) collective-permute-start(bf16[256,256]{1,0:T(8,128)(2,1)S(1)} %get-tuple-element.30), channel_id=1, source_target_pairs={{0,16},{16,32},{32,48},{48,64},{64,80},{80,96},{96,112},{112,128},... | collective-permute-start | bytes 393224 | tf_op jit(solution)/shard_map/ppermute | solution.py:64
  13.4 13.0 %copy-start = (bf16[1,256,8192]{2,1,0:T(8,128)(2,1)S(1)}, bf16[1,256,8192]{2,1,0:T(8,128)(2,1)}, u32[]{:S(2)}) copy-start(bf16[1,256,8192]{2,1,0:T(8,128)(2,1)} %param.9) | copy-start | bytes 12582916
  13.4 13.0 %copy-start.1 = (bf16[16,512]{1,0:T(8,128)(2,1)S(1)}, bf16[16,512]{1,0:T(8,128)(2,1)}, u32[]{:S(2)}) copy-start(bf16[16,512]{1,0:T(8,128)(2,1)} %refs_8_.3) | copy-start | bytes 49156
  22.0 4.4 %collective-permute-start.2 = (bf16[256,256]{1,0:T(8,128)(2,1)S(1)}, bf16[256,256]{1,0:T(8,128)(2,1)S(1)}, u32[]{:S(2)}, u32[]{:S(2)}) collective-permute-start(bf16[256,256]{1,0:T(8,128)(2,1)S(1)} %get-tuple-element.41), channel_id=1, source_target_pairs={{0,240},{16,0},{32,16},{48,32},{64,48},{80,64},{96,80},{112,96},{1... | collective-permute-start | bytes 393224 | tf_op jit(solution)/shard_map/ppermute | solution.py:64
  27.6 4.0 %collective-permute-start.3 = (bf16[16,96,128]{2,1,0:T(8,128)(2,1)S(1)}, bf16[16,96,128]{2,1,0:T(8,128)(2,1)S(1)}, u32[]{:S(2)}, u32[]{:S(2)}) collective-permute-start(bf16[16,96,128]{2,1,0:T(8,128)(2,1)S(1)} %get-tuple-element.44), channel_id=1, source_target_pairs={{0,16},{1,17},{2,18},{3,19},{4,20},{5,21},{6,22},{7,23},{8,24},{9,... | collective-permute-start | bytes 1179656 | tf_op jit(solution)/shard_map/ppermute | solution.py:59
  46.9 2.9 %collective-permute-start.4 = (bf16[96,128]{1,0:T(8,128)(2,1)S(1)}, bf16[96,128]{1,0:T(8,128)(2,1)S(1)}, u32[]{:S(2)}, u32[]{:S(2)}) collective-permute-start(bf16[96,128]{1,0:T(8,128)(2,1)S(1)} %reduce_sum.12), channel_id=1, source_target_pairs={{0,1},{1,0},{2,3},{3,2},{4,5},{5,4},{6,7},{7,6},{8,9},{9,8},{10,11... | collective-permute-start | bytes 73736 | tf_op jit(solution)/shard_map/ppermute | solution.py:59
  49.8 4.3 %collective-permute-start.5 = (bf16[96,128]{1,0:T(8,128)(2,1)S(1)}, bf16[96,128]{1,0:T(8,128)(2,1)S(1)}, u32[]{:S(2)}, u32[]{:S(2)}) collective-permute-start(bf16[96,128]{1,0:T(8,128)(2,1)S(1)} %add_convert_fusion.3), channel_id=1, source_target_pairs={{0,2},{1,3},{2,0},{3,1},{4,6},{5,7},{6,4},{7,5},{8,10},{9,11},{10,... | collective-permute-start | bytes 73736 | tf_op jit(solution)/shard_map/ppermute | solution.py:59
  54.1 6.1 %collective-permute-start.6 = (bf16[96,128]{1,0:T(8,128)(2,1)S(1)}, bf16[96,128]{1,0:T(8,128)(2,1)S(1)}, u32[]{:S(2)}, u32[]{:S(2)}) collective-permute-start(bf16[96,128]{1,0:T(8,128)(2,1)S(1)} %add_convert_fusion.2), channel_id=1, source_target_pairs={{0,7},{1,6},{2,5},{3,4},{4,3},{5,2},{6,1},{7,0},{8,15},{9,14},{10,... | collective-permute-start | bytes 73736 | tf_op jit(solution)/shard_map/ppermute | solution.py:59
  71.7 7.0 %collective-permute-start.7 = (bf16[16,96,128]{2,1,0:T(8,128)(2,1)S(1)}, bf16[16,96,128]{2,1,0:T(8,128)(2,1)S(1)}, u32[]{:S(2)}, u32[]{:S(2)}) collective-permute-start(bf16[16,96,128]{2,1,0:T(8,128)(2,1)S(1)} %all_to_all.11.ref), channel_id=1, source_target_pairs={{0,16},{1,17},{2,18},{3,19},{4,20},{5,21},{6,22},{7,23},{8,24},{9,... | collective-permute-start | bytes 1179656 | tf_op jit(solution)/shard_map/ppermute | solution.py:59

commit v3 on v2

--- a/solution.py
+++ b/solution.py
@@ -18,7 +18,7 @@
 AXES = ("seq", "dp")
 CORE_BIT = 16
 PLANE_BITS = (128, 8, 32, 64)
-DEPTH_STEPS = (1, 2, 7)
+DEPTH_STEPS = (1, 2, 6)
 CHUNKS = 32
 CHUNK_ROWS = 96
 NT = (((1,), (1,)), ((), ()))

time: 79.7 us -> 80.1 us (level)
  no operation moved by 1% of the time
where the time goes in v3:
time: 80.1 us; the launch traced here: 79.9 us
  blocking collectives  26.5 us (33%)
  starting transfers between devices  22.7 us (28%)
  Pallas kernels  22.5 us (28%)
  waiting for transfers between devices  7.24 us (9%)
    all_to_all x2, blocking collectives, exchanged(): return lax.all_to_all(value, AXES, 0, 0, axis_index_groups=groups)  26.5 us
    ppermute x5, starting transfers between devices, swapped(): return lax.ppermute(value, AXES, [(i, i ^ bit) for i in range(count)])  18.3 us
    pallas_call x2, Pallas kernels, attend(): pl.pallas_call(functools.partial(attend_kernel, far, chained), grid_spec=...  14.1 us
    ppermute x3, starting transfers between devices, shifted(): lax.ppermute(value, axis, [(i, (i + by) % devices) for i in range(devices)])  4.4 us
    ppermute x5, waiting for transfers between devices, swapped(): return lax.ppermute(value, AXES, [(i, i ^ bit) for i in range(count)])  4.35 us
    pallas_call x1, Pallas kernels, latents(): pl.pallas_call(functools.partial(latent_kernel, steps), grid_spec=pltpu.P...  4.32 us
    ppermute x3, waiting for transfers between devices, shifted(): lax.ppermute(value, axis, [(i, (i + by) % devices) for i in range(devices)])  2.89 us
    pallas_call x2, Pallas kernels, outer(): pl.pallas_call(functools.partial(outer_kernel, fresh is not None), grid_s...  2.39 us
  transfers between devices with their start and end apart: 8, of which 6 were waited for; matrix products, arithmetic and copies ran while one was open for 0% of the time, Pallas kernels for 15%

profile of v3, /device:TPU:1, one launch (start us, length us, event | category | flops | bytes accessed | tf_op | source)
XLA Modules:
  0.0 79.9 jit_solution(14762892453079364910)
XLA Ops:
  0.6 2.8 %collective-permute-start = (bf16[256,512]{1,0:T(8,128)(2,1)}, bf16[256,512]{1,0:T(8,128)(2,1)S(1)}, u32[]{:S(2)}, u32[]{:S(2)}) collective-permute-start(bf16[256,512]{1,0:T(8,128)(2,1)} %bitcast.18), channel_id=1, source_target_pairs={{0,16},{16,32},{32,48},{48,64},{64,80},{80,96},{96,112},{112,128},... | collective-permute-start | bytes 786440 | tf_op jit(solution)/shard_map/ppermute | solution.py:64
  3.4 4.3 %latents.1 = (bf16[256,32]{1,0:T(8,128)(2,1)S(1)}, bf16[32,256]{1,0:T(8,128)(2,1)S(1)}, bf16[256,512]{1,0:T(8,128)(2,1)S(1)}, bf16[256,256]{1,0:T(8,128)(2,1)S(1)}) custom-call(s32[1]{0:T(128)} %bitcast.place_ref.half_ref, bf16[256,8192]{1,0:T(8,128)(2,1)} %bitcast.11, bf16[16,8192]{1,0:T(8,128)(2,1)} %bitcast.23, bf16[16,8192]{1,0:T(8,128)(2,1)} %bitcast.24, ...), custom_call_target="tpu_custom_call" | custom-call | flops 134217728 | bytes 4194304 | tf_op jit(solution)/shard_map/latents/pallas_call | solution.py:119
  7.7 0.1 collective-permute-start.1
  7.9 5.5 %attend_near.1 = (bf16[256,4096]{1,0:T(8,128)(2,1)}, f32[16,4096]{1,0:T(8,128)S(1)}, f32[16,256]{1,0:T(8,128)S(1)}, f32[256,256]{1,0:T(8,128)S(1)}) custom-call(s32[1]{0:T(128)S(6)} %mul.7.first_ref, bf16[256,4096]{1,0:T(8,128)(2,1)S(1)} %bitcast.14, bf16[256,4096]{1,0:T(8,128)(2,1)S(1)} %bitcast.16, bf16[256,512]{1,0:T(8,128)(2,1)S(1)} %bitcast.19, ...), custom_call_target="tpu_custom_call" | custom-call | flops 1342177280 | bytes 3145728 | tf_op jit(solution)/shard_map/attend_near/pallas_call | solution.py:279
  13.4 8.6 %attend_far.1 = (bf16[256,4096]{1,0:T(8,128)(2,1)}, f32[16,4096]{1,0:T(8,128)S(1)}, f32[16,256]{1,0:T(8,128)S(1)}, f32[256,256]{1,0:T(8,128)S(1)}, bf16[256,256]{1,0:T(8,128)(2,1)S(1)}) custom-call(s32[1]{0:T(128)S(6)} %mul.6.first_ref, bf16[256,4096]{1,0:T(8,128)(2,1)S(1)} %bitcast.15, ...), custom_call_target="tpu_custom_call", output_to_operand_aliasing={{0}: (10, {}), {1}: (11, {})} | custom-call | flops 2684354560 | bytes 3145728 | tf_op jit(solution)/shard_map/attend_far/pallas_call | solution.py:279
  22.0 1.5 %collective-permute-start.2 = (bf16[256,256]{1,0:T(8,128)(2,1)S(1)}, bf16[256,256]{1,0:T(8,128)(2,1)S(1)}, u32[]{:S(2)}, u32[]{:S(2)}) collective-permute-start(bf16[256,256]{1,0:T(8,128)(2,1)S(1)} %get-tuple-element.41), channel_id=1, source_target_pairs={{0,240},{16,0},{32,16},{48,32},{64,48},{80,64},{96,80},{112,96},{1... | collective-permute-start | bytes 393224 | tf_op jit(solution)/shard_map/ppermute | solution.py:64
  23.5 2.9 %collective-permute-done.2.refs_6_ = bf16[256,256]{1,0:T(8,128)(2,1)S(1)} collective-permute-done((bf16[256,256]{1,0:T(8,128)(2,1)S(1)}, bf16[256,256]{1,0:T(8,128)(2,1)S(1)}, u32[]{:S(2)}, u32[]{:S(2)}) %collective-permute-start.2) | collective-permute-done | bytes 131104 | tf_op jit(solution)/shard_map/ppermute | solution.py:64
  26.4 1.2 %outer_first.1 = (bf16[16,96,128]{2,1,0:T(8,128)(2,1)S(1)}, bf16[32,256]{1,0:T(8,128)(2,1)S(1)}, bf16[256,256]{1,0:T(8,128)(2,1)S(1)}) custom-call(s32[1]{0:T(128)S(6)} %sub.3.half_ref, bf16[256,8192]{1,0:T(8,128)(2,1)S(1)} %bitcast.12, f32[16,4096]{1,0:T(8,128)S(1)} %get-tuple-element.37.refs_1_, ...), custom_call_target="tpu_custom_call" | custom-call | flops 67108864 | bytes 2097152 | tf_op jit(solution)/shard_map/outer_first/pallas_call | solution.py:372
  27.6 2.6 %collective-permute-start.3 = (bf16[16,96,128]{2,1,0:T(8,128)(2,1)S(1)}, bf16[16,96,128]{2,1,0:T(8,128)(2,1)S(1)}, u32[]{:S(2)}, u32[]{:S(2)}) collective-permute-start(bf16[16,96,128]{2,1,0:T(8,128)(2,1)S(1)} %get-tuple-element.44), channel_id=1, source_target_pairs={{0,16},{1,17},{2,18},{3,19},{4,20},{5,21},{6,22},{7,23},{8,24},{9,... | collective-permute-start | bytes 1179656 | tf_op jit(solution)/shard_map/ppermute | solution.py:59
  30.3 1.1 %outer_second.1 = f32[16,96,128]{2,1,0:T(8,128)S(1)} custom-call(s32[1]{0:T(128)} %bitcast.place_ref.half_ref, bf16[256,8192]{1,0:T(8,128)(2,1)S(1)} %bitcast.13, f32[16,4096]{1,0:T(8,128)S(1)} %get-tuple-element.37.refs_1_, bf16[32,256]{1,0:T(8,128)(2,1)S(1)} %get-tuple-element.32.refs_5_.refs_7_.refs_2_, bf16[256,256]{1,0:T(8,128)(2,1)S(1)} %get-tuple-element.42.refs_3_, ...), custom_call_target="tpu_custom_call" | custom-call | flops 67108864 | bytes 2097152 | tf_op jit(solution)/shard_map/outer_second/pallas_call | solution.py:372
  31.4 0.2 collective-permute-done.3
  31.6 0.1 add_convert_fusion
  31.7 15.1 %all_to_all.10 = bf16[16,96,128]{2,1,0:T(8,128)(2,1)S(1)} all-to-all(bf16[16,96,128]{2,1,0:T(8,128)(2,1)S(1)} %add_convert_fusion), channel_id=1, replica_groups={{0,128,8,136,32,160,40,168,64,192,72,200,96,224,104,232},{1,129,9,137,3..., dimensions={0} | all-to-all | bytes 786432 | tf_op jit(solution)/shard_map/all_to_all | solution.py:45
  46.9 1.7 %collective-permute-start.4 = (bf16[96,128]{1,0:T(8,128)(2,1)S(1)}, bf16[96,128]{1,0:T(8,128)(2,1)S(1)}, u32[]{:S(2)}, u32[]{:S(2)}) collective-permute-start(bf16[96,128]{1,0:T(8,128)(2,1)S(1)} %reduce_sum.12), channel_id=1, source_target_pairs={{0,1},{1,0},{2,3},{3,2},{4,5},{5,4},{6,7},{7,6},{8,9},{9,8},{10,11... | collective-permute-start | bytes 73736 | tf_op jit(solution)/shard_map/ppermute | solution.py:59
  48.6 1.2 %collective-permute-done.4 = bf16[96,128]{1,0:T(8,128)(2,1)S(1)} collective-permute-done((bf16[96,128]{1,0:T(8,128)(2,1)S(1)}, bf16[96,128]{1,0:T(8,128)(2,1)S(1)}, u32[]{:S(2)}, u32[]{:S(2)}) %collective-permute-start.4) | collective-permute-done | bytes 24608 | tf_op jit(solution)/shard_map/ppermute | solution.py:59
  49.8 3.1 %collective-permute-start.5 = (bf16[96,128]{1,0:T(8,128)(2,1)S(1)}, bf16[96,128]{1,0:T(8,128)(2,1)S(1)}, u32[]{:S(2)}, u32[]{:S(2)}) collective-permute-start(bf16[96,128]{1,0:T(8,128)(2,1)S(1)} %add_convert_fusion.3), channel_id=1, source_target_pairs={{0,2},{1,3},{2,0},{3,1},{4,6},{5,7},{6,4},{7,5},{8,10},{9,11},{10,... | collective-permute-start | bytes 73736 | tf_op jit(solution)/shard_map/ppermute | solution.py:59
  52.9 1.2 %collective-permute-done.5 = bf16[96,128]{1,0:T(8,128)(2,1)S(1)} collective-permute-done((bf16[96,128]{1,0:T(8,128)(2,1)S(1)}, bf16[96,128]{1,0:T(8,128)(2,1)S(1)}, u32[]{:S(2)}, u32[]{:S(2)}) %collective-permute-start.5) | collective-permute-done | bytes 24608 | tf_op jit(solution)/shard_map/ppermute | solution.py:59
  54.1 5.3 %collective-permute-start.6 = (bf16[96,128]{1,0:T(8,128)(2,1)S(1)}, bf16[96,128]{1,0:T(8,128)(2,1)S(1)}, u32[]{:S(2)}, u32[]{:S(2)}) collective-permute-start(bf16[96,128]{1,0:T(8,128)(2,1)S(1)} %add_convert_fusion.2), channel_id=1, source_target_pairs={{0,6},{1,7},{2,4},{3,5},{4,2},{5,3},{6,0},{7,1},{8,14},{9,15},{10,... | collective-permute-start | bytes 73736 | tf_op jit(solution)/shard_map/ppermute | solution.py:59
  59.4 1.2 %collective-permute-done.6 = bf16[96,128]{1,0:T(8,128)(2,1)S(1)} collective-permute-done((bf16[96,128]{1,0:T(8,128)(2,1)S(1)}, bf16[96,128]{1,0:T(8,128)(2,1)S(1)}, u32[]{:S(2)}, u32[]{:S(2)}) %collective-permute-start.6) | collective-permute-done | bytes 24608 | tf_op jit(solution)/shard_map/ppermute | solution.py:59
  60.7 11.4 %all_to_all.11.ref = bf16[16,96,128]{2,1,0:T(8,128)(2,1)S(1)} all-to-all(bf16[16,96,128]{2,1,0:T(8,128)(2,1)S(1)} %broadcast_in_dim.10), channel_id=1, replica_groups={{0,128,8,136,32,160,40,168,64,192,72,200,96,224,104,232},{1,129,9,137,3..., dimensions={0} | all-to-all | bytes 786432 | tf_op jit(solution)/shard_map/all_to_all | solution.py:45
  72.1 5.6 %collective-permute-start.7 = (bf16[16,96,128]{2,1,0:T(8,128)(2,1)S(1)}, bf16[16,96,128]{2,1,0:T(8,128)(2,1)S(1)}, u32[]{:S(2)}, u32[]{:S(2)}) collective-permute-start(bf16[16,96,128]{2,1,0:T(8,128)(2,1)S(1)} %all_to_all.11.ref), channel_id=1, source_target_pairs={{0,16},{1,17},{2,18},{3,19},{4,20},{5,21},{6,22},{7,23},{8,24},{9,... | collective-permute-start | bytes 1179656 | tf_op jit(solution)/shard_map/ppermute | solution.py:59
  77.7 0.9 %unpack_own.1 = (f32[16,8192]{1,0:T(8,128)}, f32[16,8192]{1,0:T(8,128)}, f32[16,4096]{1,0:T(8,128)}, f32[16,512]{1,0:T(8,128)}) custom-call(s32[1]{0:T(128)} %bitcast.place_ref.half_ref, bf16[16,96,128]{2,1,0:T(8,128)(2,1)S(1)} %all_to_all.11.ref), custom_call_target="tpu_custom_call" | custom-call | bytes 1048576 | tf_op jit(solution)/shard_map/unpack_own/pallas_call | solution.py:407
  78.6 0.5 collective-permute-done.7.ref
  79.1 0.9 %unpack_other.1 = (f32[16,8192]{1,0:T(8,128)}, f32[16,8192]{1,0:T(8,128)}, f32[16,4096]{1,0:T(8,128)}, f32[16,512]{1,0:T(8,128)}) custom-call(s32[1]{0:T(128)S(6)} %sub.3.half_ref, bf16[16,96,128]{2,1,0:T(8,128)(2,1)S(1)} %collective-permute-done.7.ref, ...), custom_call_target="tpu_custom_call", output_to_operand_aliasing={{0}: (2, {}), {1}: (3, {}), {2}: (4, {}), {3}: (5, {})} | custom-call | bytes 1048576 | tf_op jit(solution)/shard_map/unpack_other/pallas_call | solution.py:407
  (19 shorter events, 0.2 us)
Async XLA Ops:
  0.6 12.8 %collective-permute-start = (bf16[256,512]{1,0:T(8,128)(2,1)}, bf16[256,512]{1,0:T(8,128)(2,1)S(1)}, u32[]{:S(2)}, u32[]{:S(2)}) collective-permute-start(bf16[256,512]{1,0:T(8,128)(2,1)} %bitcast.18), channel_id=1, source_target_pairs={{0,16},{16,32},{32,48},{48,64},{64,80},{80,96},{96,112},{112,128},... | collective-permute-start | bytes 786440 | tf_op jit(solution)/shard_map/ppermute | solution.py:64
  3.4 4.5 %copy-start.2 = (bf16[1,256,4096]{2,1,0:T(8,128)(2,1)S(1)}, bf16[1,256,4096]{2,1,0:T(8,128)(2,1)}, u32[]{:S(2)}) copy-start(bf16[1,256,4096]{2,1,0:T(8,128)(2,1)} %param.10) | copy-start | bytes 6291460
  3.4 4.5 %copy-start.3 = (bf16[1,256,4096]{2,1,0:T(8,128)(2,1)S(1)}, bf16[1,256,4096]{2,1,0:T(8,128)(2,1)}, u32[]{:S(2)}) copy-start(bf16[1,256,4096]{2,1,0:T(8,128)(2,1)} %param.17) | copy-start | bytes 6291460
  3.4 4.5 %copy-start.4 = (bf16[1,256,512]{2,1,0:T(8,128)(2,1)S(1)}, bf16[1,256,512]{2,1,0:T(8,128)(2,1)}, u32[]{:S(2)}) copy-start(bf16[1,256,512]{2,1,0:T(8,128)(2,1)} %param.11) | copy-start | bytes 786436
  3.4 4.5 %copy-start.5 = (bf16[16,4096]{1,0:T(8,128)(2,1)S(1)}, bf16[16,4096]{1,0:T(8,128)(2,1)}, u32[]{:S(2)}) copy-start(bf16[16,4096]{1,0:T(8,128)(2,1)} %refs_8_.2) | copy-start | bytes 393220
  7.7 5.7 %collective-permute-start.1 = (bf16[256,256]{1,0:T(8,128)(2,1)S(1)}, bf16[256,256]{1,0:T(8,128)(2,1)S(1)}, u32[]{:S(2)}, u32[]{:S(2)}) collective-permute-start(bf16[256,256]{1,0:T(8,128)(2,1)S(1)} %get-tuple-element.30), channel_id=1, source_target_pairs={{0,16},{16,32},{32,48},{48,64},{64,80},{80,96},{96,112},{112,128},... | collective-permute-start | bytes 393224 | tf_op jit(solution)/shard_map/ppermute | solution.py:64
  13.4 13.0 %copy-start = (bf16[1,256,8192]{2,1,0:T(8,128)(2,1)S(1)}, bf16[1,256,8192]{2,1,0:T(8,128)(2,1)}, u32[]{:S(2)}) copy-start(bf16[1,256,8192]{2,1,0:T(8,128)(2,1)} %param.9) | copy-start | bytes 12582916
  13.4 13.0 %copy-start.1 = (bf16[16,512]{1,0:T(8,128)(2,1)S(1)}, bf16[16,512]{1,0:T(8,128)(2,1)}, u32[]{:S(2)}) copy-start(bf16[16,512]{1,0:T(8,128)(2,1)} %refs_8_.3) | copy-start | bytes 49156
  22.0 4.4 %collective-permute-start.2 = (bf16[256,256]{1,0:T(8,128)(2,1)S(1)}, bf16[256,256]{1,0:T(8,128)(2,1)S(1)}, u32[]{:S(2)}, u32[]{:S(2)}) collective-permute-start(bf16[256,256]{1,0:T(8,128)(2,1)S(1)} %get-tuple-element.41), channel_id=1, source_target_pairs={{0,240},{16,0},{32,16},{48,32},{64,48},{80,64},{96,80},{112,96},{1... | collective-permute-start | bytes 393224 | tf_op jit(solution)/shard_map/ppermute | solution.py:64
  27.6 4.0 %collective-permute-start.3 = (bf16[16,96,128]{2,1,0:T(8,128)(2,1)S(1)}, bf16[16,96,128]{2,1,0:T(8,128)(2,1)S(1)}, u32[]{:S(2)}, u32[]{:S(2)}) collective-permute-start(bf16[16,96,128]{2,1,0:T(8,128)(2,1)S(1)} %get-tuple-element.44), channel_id=1, source_target_pairs={{0,16},{1,17},{2,18},{3,19},{4,20},{5,21},{6,22},{7,23},{8,24},{9,... | collective-permute-start | bytes 1179656 | tf_op jit(solution)/shard_map/ppermute | solution.py:59
  46.9 2.9 %collective-permute-start.4 = (bf16[96,128]{1,0:T(8,128)(2,1)S(1)}, bf16[96,128]{1,0:T(8,128)(2,1)S(1)}, u32[]{:S(2)}, u32[]{:S(2)}) collective-permute-start(bf16[96,128]{1,0:T(8,128)(2,1)S(1)} %reduce_sum.12), channel_id=1, source_target_pairs={{0,1},{1,0},{2,3},{3,2},{4,5},{5,4},{6,7},{7,6},{8,9},{9,8},{10,11... | collective-permute-start | bytes 73736 | tf_op jit(solution)/shard_map/ppermute | solution.py:59
  49.8 4.3 %collective-permute-start.5 = (bf16[96,128]{1,0:T(8,128)(2,1)S(1)}, bf16[96,128]{1,0:T(8,128)(2,1)S(1)}, u32[]{:S(2)}, u32[]{:S(2)}) collective-permute-start(bf16[96,128]{1,0:T(8,128)(2,1)S(1)} %add_convert_fusion.3), channel_id=1, source_target_pairs={{0,2},{1,3},{2,0},{3,1},{4,6},{5,7},{6,4},{7,5},{8,10},{9,11},{10,... | collective-permute-start | bytes 73736 | tf_op jit(solution)/shard_map/ppermute | solution.py:59
  54.1 6.5 %collective-permute-start.6 = (bf16[96,128]{1,0:T(8,128)(2,1)S(1)}, bf16[96,128]{1,0:T(8,128)(2,1)S(1)}, u32[]{:S(2)}, u32[]{:S(2)}) collective-permute-start(bf16[96,128]{1,0:T(8,128)(2,1)S(1)} %add_convert_fusion.2), channel_id=1, source_target_pairs={{0,6},{1,7},{2,4},{3,5},{4,2},{5,3},{6,0},{7,1},{8,14},{9,15},{10,... | collective-permute-start | bytes 73736 | tf_op jit(solution)/shard_map/ppermute | solution.py:59
  72.1 7.0 %collective-permute-start.7 = (bf16[16,96,128]{2,1,0:T(8,128)(2,1)S(1)}, bf16[16,96,128]{2,1,0:T(8,128)(2,1)S(1)}, u32[]{:S(2)}, u32[]{:S(2)}) collective-permute-start(bf16[16,96,128]{2,1,0:T(8,128)(2,1)S(1)} %all_to_all.11.ref), channel_id=1, source_target_pairs={{0,16},{1,17},{2,18},{3,19},{4,20},{5,21},{6,22},{7,23},{8,24},{9,... | collective-permute-start | bytes 1179656 | tf_op jit(solution)/shard_map/ppermute | solution.py:59
